TPU v7x, 128 devices: a whole 4x4x4 slice. The times are simulated.
128 devices in a mesh: sub: 32 (over y_lo, z, x), lev: 4 (over y_hi, core).
Axes of the slice: x: 4, y: 4 (y_hi: 2, y_lo: 2; y = y_hi * 2 + y_lo), z: 4, core: 2. Of those that a mesh axis runs over, the one named last changes fastest.
Arguments:
- wind_u: float32 [16, 8192, 256], P('lev', 'sub'), may hold values from -6 to 6
- wind_v: float32 [16, 8192, 256], P('lev', 'sub'), may hold values from -6 to 6
- vertical: float32 [16, 8192, 256], P('lev', 'sub'), may hold values from -6 to 6
- spacing_x: float32 [8192, 256], P('sub'), may hold values from 0.5 to 2
- spacing_y: float32 [8192, 256], P('sub'), may hold values from 0.5 to 2
- coriolis: float32 [8192, 256], P('sub'), may hold values from -4 to 4
- edge_source: int32 [32, 4], P('sub'), may hold values from 0 to 127
- edge_turns: int32 [32, 4], P('sub'), may hold values from 0 to 3
- route_owner: int32 [16384, 2], P('sub'), may hold values from 0 to 31, all different within a row; in each aligned block of 512 rows (0 to 511, 512 to 1023, ...) at most 64 rows name the same one
- route_window: int32 [16384, 2], P('sub'), may hold values from 0 to 3
- remap_weights: bfloat16 [16384, 2, 128, 128], P('sub'), may hold values from 0 to 6.1035156e-05
Outputs:
- tendencies: float32 [2, 16, 8192, 256], P(None, 'lev', 'sub')
- remapped: float32 [2, 16, 16384], P(None, 'lev', 'sub')
Inputs may be any that keep to these rules, and one draw needn't show every extreme that they name: `route_owner`: each row names two different owners; among the rows of one subdomain at most 64 name one owner, a bound that some block reaches.
All inputs are finite; a program needn't handle non-finite values.
Results may differ from a plain program's by a relative error of at most 0.0031.
Values sent between devices are 32-bit elements; how exact they have to be, the bound alone decides.
No kernel may reach another device: no remote copies, remote signals or barrier semaphores. Data moves between devices by JAX's collectives and lax.ppermute only.
A program may use at most 128 MiB of HBM per device.

v0:
```python
import jax
import jax.numpy as jnp
from jax import lax
from jax.sharding import PartitionSpec as P

WINDOWS = 4


def with_halo(cells, sides, width):
    for axis, dim in sides:
        count = lax.axis_size(axis)
        ends = count - 1
        head = lax.slice_in_dim(cells, 0, width, axis=dim)
        tail = lax.slice_in_dim(cells, cells.shape[dim] - width, cells.shape[dim], axis=dim)
        cells = jnp.concatenate(
            [
                lax.ppermute(tail, axis, [(i, (i + 1) % count) for i in range(ends)]),
                cells,
                lax.ppermute(head, axis, [((i + 1) % count, i) for i in range(ends)]),
            ],
            axis=dim,
        )
    return cells


def side_rows(field):
    return jnp.stack([field[:, :, 0], field[:, :, -1], field[:, 0, :], field[:, -1, :]], axis=0)


def turn_edges(edge_u, edge_v, turns):
    cosine = (turns == 0).astype(jnp.float32) - (turns == 2).astype(jnp.float32)
    sine = (turns == 1).astype(jnp.float32) - (turns == 3).astype(jnp.float32)
    new_u = cosine * edge_u - sine * edge_v
    new_v = sine * edge_u + cosine * edge_v
    odd = turns % 2 == 1
    return (jnp.where(odd, new_u[..., ::-1], new_u), jnp.where(odd, new_v[..., ::-1], new_v))


def fill_halo(field, halo):
    padded = jnp.pad(field, ((0, 0), (1, 1), (1, 1)))
    padded = padded.at[:, 1:-1, 0].set(halo[0])
    padded = padded.at[:, 1:-1, -1].set(halo[1])
    padded = padded.at[:, 0, 1:-1].set(halo[2])
    padded = padded.at[:, -1, 1:-1].set(halo[3])
    return padded


def per_device(
    wind_u,
    wind_v,
    vertical,
    spacing_x,
    spacing_y,
    coriolis,
    edge_source,
    edge_turns,
    route_owner,
    route_window,
    remap_weights,
):
    levels_here, width_cells, _ = wind_u.shape
    owners = lax.axis_size("sub")
    edges = jnp.stack([side_rows(wind_u), side_rows(wind_v)], axis=1)
    wanted = edge_source[0]
    piece = lax.all_gather(edges, "sub", axis=0, tiled=True)
    edge_ids = jnp.arange(piece.shape[0], dtype=jnp.int32)
    match = (wanted[:, None] == edge_ids[None, :]).astype(jnp.float32)
    halo_vals = jnp.einsum("sr,rclp->sclp", match, piece, precision=lax.Precision.HIGHEST)
    halo_u, halo_v = turn_edges(halo_vals[:, 0], halo_vals[:, 1], edge_turns[0][:, None, None])
    stacked = jnp.stack([wind_u, wind_v], axis=0)
    column = with_halo(stacked, (("lev", 1),), 1)
    padded_u = fill_halo(wind_u, halo_u)
    padded_v = fill_halo(wind_v, halo_v)
    kinetic = 0.5 * (padded_u * padded_u + padded_v * padded_v)
    vorticity = (
        (padded_v[:, 1:-1, 2:] - padded_v[:, 1:-1, :-2]) / (2.0 * spacing_x)
        - (padded_u[:, 2:, 1:-1] - padded_u[:, :-2, 1:-1]) / (2.0 * spacing_y)
        + coriolis
    )
    tend_u = (
        vorticity * wind_v
        - (kinetic[:, 1:-1, 2:] - kinetic[:, 1:-1, :-2]) / (2.0 * spacing_x)
        - vertical * (column[0, 2:] - column[0, :-2]) * 0.5
    )
    tend_v = (
        -vorticity * wind_u
        - (kinetic[:, 2:, 1:-1] - kinetic[:, :-2, 1:-1]) / (2.0 * spacing_y)
        - vertical * (column[1, 2:] - column[1, :-2]) * 0.5
    )
    tendencies = jnp.stack([tend_u, tend_v], 0)
    block_count = width_cells * width_cells // 128
    blocks = (
        tendencies.astype(jnp.bfloat16)
        .reshape(2 * levels_here, block_count, 128)
        .transpose(1, 0, 2)
    )
    partial_value = jnp.einsum(
        "brq,btqp->btrp", blocks, remap_weights, preferred_element_type=jnp.float32
    )
    ones_col = jnp.ones((128,), jnp.bfloat16)
    weight_sum = jnp.einsum(
        "btqp,q->btp", remap_weights, ones_col, preferred_element_type=jnp.float32
    )
    pair_count = 2 * block_count
    flat_part = partial_value.reshape(pair_count, 2 * levels_here, 128)
    flat_sum = weight_sum.reshape(pair_count, 128)
    owner_flat = route_owner.reshape(-1)
    window_flat = route_window.reshape(-1)
    windows = WINDOWS
    target = owner_flat * windows + window_flat
    send_part = (
        jnp.zeros((owners * windows, 2 * levels_here, 128), jnp.float32).at[target].add(flat_part)
    )
    send_sum = jnp.zeros((owners * windows, 128), jnp.float32).at[target].add(flat_sum)
    got_part, got_sum = (
        lax.all_to_all(
            send_part.reshape(owners, windows, 2 * levels_here, 128),
            "sub",
            split_axis=0,
            concat_axis=0,
            tiled=True,
        ),
        lax.all_to_all(
            send_sum.reshape(owners, windows, 128), "sub", split_axis=0, concat_axis=0, tiled=True
        ),
    )
    accumulated = jnp.sum(got_part, axis=0).transpose(1, 0, 2)
    fraction = jnp.sum(got_sum, axis=0)
    result = accumulated / jnp.maximum(fraction, 1.0)[None, :, :]
    result = result.reshape(2, levels_here, windows * 128)
    return (tendencies, result)


def solution(mesh):
    placed = (
        P("lev", "sub", None),
        P("lev", "sub", None),
        P("lev", "sub", None),
        P("sub", None),
        P("sub", None),
        P("sub", None),
        P("sub", None),
        P("sub", None),
        P("sub", None),
        P("sub", None),
        P("sub", None, None, None),
    )
    return jax.shard_map(
        per_device,
        mesh=mesh,
        in_specs=placed,
        out_specs=(P(None, "lev", "sub", None), P(None, "lev", "sub")),
        check_vma=False,
    )
```

profile of v0, /device:TPU:0, one launch (start us, length us, event | category | flops | bytes accessed | tf_op | source)
XLA Modules:
  0.0 357.6 jit_solution(6140539710538700923)
XLA Ops:
  8.1 1.4 fusion.38
  9.5 1.1 fusion.40
  11.0 1.2 copy.87
  12.3 1.2 copy.86
  14.2 1.1 pad_maximum_fusion.6
  15.3 1.3 collective-permute-start
  16.5 3.1 collective-permute-start.1
  20.0 13.6 %fusion.33 = f32[1,1024,128]{2,0,1:T(1,128)} fusion(bf16[1024,128,128]{1,2,0:T(8,128)(2,1)} %bitcast.106), kind=kOutput, calls=%fused_computation.82 | convolution fusion | flops 33554432 | bytes 34078720 | tf_op jit(solution)/shard_map/btqp,q->btp/dot_general | solution.py:101
  33.7 7.0 %scatter_custom_fusion.1 = f32[128,128]{1,0:T(8,128)} fusion(s32[1024]{0:T(1024)S(1)} %bitcast.115, f32[1024,128]{1,0:T(8,128)} %bitcast.114, f32[]{:T(128)} %constant.233.clone.1), kind=kCustom, calls=%fused_computation.42 | custom fusion | flops 131072 | bytes 66048 | tf_op jit(solution)/shard_map/scatter-add | solution.py:114
  40.7 9.5 %all-to-all-start.1 = ((f32[32,4,128]{2,1,0:T(4,128)}), f32[32,4,128]{2,1,0:T(4,128)S(1)}, u32[]{:S(2)}, u32[]{:S(2)}) async-start(f32[32,4,128]{2,1,0:T(4,128)} %bitcast.43), calls=%async_computation.1 | async-start | bytes 131072 | tf_op jit(solution)/shard_map/all_to_all | solution.py:123
  50.1 1.7 pad.40
  51.9 1.7 pad.39
  55.6 112.3 %all-gather.2.cloned.1.call-done = f32[128,2,4,256]{3,2,1,0:T(4,128)} async-done(((f32[4,2,4,256]{3,2,1,0:T(4,128)}), f32[128,2,4,256]{3,2,1,0:T(4,128)}) %all-gather.2.cloned.1.call-update) | async-done | bytes 1048592 | tf_op jit(solution)/shard_map/all_gather | solution.py:65
  167.9 1.9 fusion.22
  171.1 1.1 copy.72
  173.2 1.0 copy.70
  174.2 1.0 copy.71
  175.2 3.3 scatter.34
  178.6 3.9 %scatter.35 = f32[4,258,258]{2,1,0:T(8,128)} dynamic-update-slice(f32[4,258,258]{2,1,0:T(8,128)} %scatter.34, f32[4,256,1]{2,1,0:T(8,128)} %copy.73, s32[]{:T(128)} %constant.234.clone.1, s32[]{:T(128)} %constant.235.clone.1, s32[]{:T(128)} %constant.238.clone.1) | dynamic-update-slice | bytes 8196 | tf_op jit(solution)/shard_map/scatter | solution.py:42
  182.5 3.3 scatter.36
  185.7 2.0 scatter.39
  187.7 3.3 scatter.26
  191.0 3.9 %scatter.29 = f32[4,258,258]{2,1,0:T(8,128)} dynamic-update-slice(f32[4,258,258]{2,1,0:T(8,128)} %scatter.26, f32[4,256,1]{2,1,0:T(8,128)} %copy.71, s32[]{:T(128)} %constant.234.clone.1, s32[]{:T(128)} %constant.235.clone.1, s32[]{:T(128)} %constant.238.clone.1) | dynamic-update-slice | bytes 8196 | tf_op jit(solution)/shard_map/scatter | solution.py:42
  194.9 3.3 scatter.30
  198.2 2.0 scatter.31
  200.2 2.3 add_multiply_fusion
  203.5 1.5 fusion.12
  205.8 1.6 fusion.36
  207.8 15.2 %fusion.19 = f32[512,8,2,128]{3,1,2,0:T(8,128)} fusion(bf16[512,2,128,128]{3,2,1,0:T(8,128)(2,1)} %param.37, bf16[8,512,128]{2,1,0:T(8,128)(2,1)S(1)} %convert_element_type.48), kind=kOutput, calls=%fused_computation.32 | convolution fusion | flops 268435456 | bytes 38797312 | tf_op jit(solution)/shard_map/brq,btqp->btrp/dot_general | solution.py:97
  223.8 109.1 %scatter_fusion = f32[128,8,128]{2,1,0:T(8,128)} fusion(f32[128,8,128]{2,1,0:T(8,128)} %broadcast_in_dim.30, s32[1024]{0:T(1024)S(1)} %bitcast.116, f32[1024,8,128]{2,1,0:T(8,128)} %bitcast.113), kind=kCustom, calls=%fused_computation | custom fusion | flops 1048576 | bytes 12587008 | tf_op jit(solution)/shard_map/scatter-add | solution.py:112
  332.9 7.1 %all-to-all-start = ((f32[32,4,8,128]{3,2,1,0:T(8,128)}), f32[32,4,8,128]{3,2,1,0:T(8,128)S(1)}, u32[]{:S(2)}, u32[]{:S(2)}) async-start(f32[32,4,8,128]{3,2,1,0:T(8,128)} %bitcast.38), calls=%async_computation | async-start | bytes 1048576 | tf_op jit(solution)/shard_map/all_to_all | solution.py:116
  340.1 10.0 %all-to-all-done = f32[32,4,8,128]{3,2,1,0:T(8,128)S(1)} async-done(((f32[32,4,8,128]{3,2,1,0:T(8,128)}), f32[32,4,8,128]{3,2,1,0:T(8,128)S(1)}, u32[]{:S(2)}, u32[]{:S(2)}) %all-to-all-start) | async-done | bytes 524320 | tf_op jit(solution)/shard_map/all_to_all | solution.py:116
  (69 shorter events, 10.4 us)
Async XLA Ops:
  7.2 2.3 copy-start
  7.2 160.7 %all-gather.2.cloned.1.call-start = ((), (), s32[]{:S(2)}) async-start(), calls=%async_computation.2 | async-start | bytes 1081344 | tf_op jit(solution)/shard_map/all_gather | solution.py:65
  10.6 3.6 copy-start.1
  13.5 6.1 %copy-start.11 = (s32[512,2]{0,1:T(2,128)S(1)}, s32[512,2]{0,1:T(2,128)}, u32[]{:S(2)}) copy-start(s32[512,2]{0,1:T(2,128)} %param.36) | copy-start | bytes 12292
  13.5 6.1 %copy-start.12 = (s32[512,2]{0,1:T(2,128)S(1)}, s32[512,2]{0,1:T(2,128)}, u32[]{:S(2)}) copy-start(s32[512,2]{0,1:T(2,128)} %param.35) | copy-start | bytes 12292
  15.3 187.3 %collective-permute-start = (f32[2,1,256,256]{3,2,1,0:T(8,128)}, f32[2,1,256,256]{3,2,1,0:T(8,128)S(1)}, u32[]{:S(2)}, u32[]{:S(2)}) collective-permute-start(f32[2,1,256,256]{3,2,1,0:T(8,128)} %get-tuple-element.102), channel_id=1, source_target_pairs={{1,0},{2,1},{3,2},{5,4},{6,5},{7,6},{9,8},{10,9},{11,10},{13,12},{... | collective-permute-start | bytes 1572872 | tf_op jit(solution)/shard_map/ppermute | solution.py:19
  16.5 186.0 %collective-permute-start.1 = (f32[2,1,256,256]{3,2,1,0:T(8,128)}, f32[2,1,256,256]{3,2,1,0:T(8,128)S(1)}, u32[]{:S(2)}, u32[]{:S(2)}) collective-permute-start(f32[2,1,256,256]{3,2,1,0:T(8,128)} %get-tuple-element.103), channel_id=1, source_target_pairs={{0,1},{1,2},{2,3},{4,5},{5,6},{6,7},{8,9},{9,10},{10,11},{12,13},{... | collective-permute-start | bytes 1572872 | tf_op jit(solution)/shard_map/ppermute | solution.py:17
  20.0 13.7 %copy-start.9 = (s32[1024,1]{0,1:T(1,128)}, s32[1024,1]{0,1:T(1,128)S(1)}, u32[]{:S(2)}) copy-start(s32[1024,1]{0,1:T(1,128)S(1)} %compare_select_fusion) | copy-start | bytes 12292
  40.7 292.3 %all-to-all-start.1 = ((f32[32,4,128]{2,1,0:T(4,128)}), f32[32,4,128]{2,1,0:T(4,128)S(1)}, u32[]{:S(2)}, u32[]{:S(2)}) async-start(f32[32,4,128]{2,1,0:T(4,128)} %bitcast.43), calls=%async_computation.1 | async-start | bytes 131072 | tf_op jit(solution)/shard_map/all_to_all | solution.py:123
  51.8 2.3 copy-start.14
  51.9 3.0 copy-start.7
  51.9 3.0 copy-start.8
  51.9 116.0 %copy-start.13 = (s32[1,4]{1,0:T(1,128)S(1)}, s32[1,4]{1,0:T(1,128)}, u32[]{:S(2)}) copy-start(s32[1,4]{1,0:T(1,128)} %param.33) | copy-start | bytes 52
  200.2 2.4 copy-start.2
  200.2 2.9 copy-start.3
  200.2 3.2 copy-start.4
  200.2 3.2 copy-start.5
  200.2 3.3 copy-start.6
  207.8 16.0 %copy-start.10 = (s32[1024,1]{0,1:T(1,128)S(1)}, s32[1024,1]{0,1:T(1,128)}, u32[]{:S(2)}) copy-start(s32[1024,1]{0,1:T(1,128)} %copy-done.9) | copy-start | bytes 12292
  332.9 17.1 %all-to-all-start = ((f32[32,4,8,128]{3,2,1,0:T(8,128)}), f32[32,4,8,128]{3,2,1,0:T(8,128)S(1)}, u32[]{:S(2)}, u32[]{:S(2)}) async-start(f32[32,4,8,128]{3,2,1,0:T(8,128)} %bitcast.38), calls=%async_computation | async-start | bytes 1048576 | tf_op jit(solution)/shard_map/all_to_all | solution.py:116
Sparse Core Ops, SparseCore 0:
  14.3 153.5 all-gather.1
where the time goes:
time: 362 us; the launch traced here: 358 us
  other arithmetic  126 us (35%)
  waiting for transfers between devices  122 us (34%)
  local copies, waits for them, and re-layouts  43.1 us (12%)
  matrix products  30.7 us (8%)
  starting transfers between devices  21 us (6%)
  between operations  14.3 us (4%)
    all_gather x1, waiting for transfers between devices, per_device(): piece = lax.all_gather(edges, 'sub', axis=0, tiled=True)  112 us
    scatter-add x1, other arithmetic, per_device(): jnp.zeros((owners * windows, 2 * levels_here, 128), jnp.float32).at[target]  109 us
    dot_general x1, matrix products, per_device(): jnp.einsum('brq,btqp->btrp', blocks, remap_weights, preferred_element_typ...  15.2 us
    dot_general x1, matrix products, per_device(): jnp.einsum('btqp,q->btp', remap_weights, ones_col, preferred_element_type...  13.6 us
    all_to_all x1, waiting for transfers between devices, per_device(): lax.all_to_all(send_part.reshape(owners, windows, 2 * levels_here, 128),...  9.97 us
    all_to_all x1, starting transfers between devices, per_device(): lax.all_to_all(send_sum.reshape(owners, windows, 128), 'sub', split_axis=...  9.47 us
    scatter x2, local copies, waits for them, and re-layouts, fill_halo(): padded = padded.at[:, 1:-1, -1].set(halo[1])  7.79 us
  transfers between devices with their start and end apart: 5, of which 2 were waited for; matrix products, arithmetic and copies ran while one was open for 54% of the time, Pallas kernels for 0%

commit v1 on v0

v1 whole, which is shorter than its diff:
```python
import jax
import jax.numpy as jnp
from jax import lax
from jax.experimental import pallas as pl
from jax.experimental.pallas import tpu as pltpu
from jax.sharding import PartitionSpec as P

WINDOWS = 4
CS = 256
LANES = 128
CHUNK = 16
ACCS = 4
GROUP = 32
AHEAD = 4
F32 = jnp.float32
BF16 = jnp.bfloat16


def vmem():
    return pl.BlockSpec(memory_space=pltpu.VMEM)


def smem():
    return pl.BlockSpec(memory_space=pltpu.SMEM)


def hbm():
    return pl.BlockSpec(memory_space=pltpu.HBM)


def in_hbm(x):
    return pltpu.with_memory_space_constraint(x, pltpu.HBM)


def params(mib):
    return pltpu.CompilerParams(vmem_limit_bytes=mib * 1024 * 1024)


def cost(flops, size):
    return pl.CostEstimate(flops=flops, bytes_accessed=size, transcendentals=0)


def level_kernel(wind_u, wind_v, up_ref, down_ref, token_ref, held, in_sems, out_sems):
    loads, sends = [], []
    for comp, wind in enumerate((wind_u, wind_v)):
        for k, (level, out) in enumerate(((3, up_ref), (0, down_ref))):
            for half in (0, 1):
                n = 4 * comp + 2 * k + half
                rows = pl.ds(half * (CS // 2), CS // 2)
                spot = held.at[n]
                loads.append(pltpu.make_async_copy(wind.at[level, rows], spot, in_sems.at[n]))
                sends.append(pltpu.make_async_copy(spot, out.at[comp, rows], out_sems.at[n]))
    for load in loads:
        load.start()
    token_ref[...] = jnp.zeros_like(token_ref)
    for load, send in zip(loads, sends):
        load.wait()
        send.start()
    for send in sends:
        send.wait()


def take_levels(wind_u, wind_v):
    return pl.pallas_call(
        level_kernel,
        out_shape=(
            pltpu.HBM((2, CS, CS), F32),
            pltpu.HBM((2, CS, CS), F32),
            jax.ShapeDtypeStruct((8, LANES), F32),
        ),
        in_specs=[hbm(), hbm()],
        out_specs=(hbm(), hbm(), vmem()),
        scratch_shapes=[
            pltpu.VMEM((8, CS // 2, CS), F32),
            pltpu.SemaphoreType.DMA((8,)),
            pltpu.SemaphoreType.DMA((8,)),
        ],
        compiler_params=params(2),
        cost_estimate=cost(1000, 2 << 20),
        name="outer_levels",
    )(in_hbm(wind_u), in_hbm(wind_v))


def edge_kernel(wind_u, wind_v, token_ref, edges_ref, own_ref, u_ref, v_ref, held, sems, out_sems):
    del token_ref
    loads = []
    for comp, (wind, ref) in enumerate(((wind_u, u_ref), (wind_v, v_ref))):
        for level in range(4):
            sem = sems.at[4 * comp + level]
            loads.append(pltpu.make_async_copy(wind.at[level], ref.at[level], sem))
    for load in loads:
        load.start()
    lane = lax.broadcasted_iota(jnp.int32, (CS, LANES), 1)
    columns = jnp.zeros((CS, LANES), F32)
    for comp, ref in enumerate((u_ref, v_ref)):
        for level in range(4):
            loads[4 * comp + level].wait()
            for side in (0, 1):
                at = 0 if side == 0 else CS - 1
                column = ref[level, :, pl.ds(at, 1)]
                columns = jnp.where(lane == side * 8 + comp * 4 + level, column, columns)
    held[0:16, :] = jnp.transpose(columns)[0:16, :]
    for comp, ref in enumerate((u_ref, v_ref)):
        held[16 + 4 * comp : 20 + 4 * comp, :] = ref[:, 0, :]
        held[24 + 4 * comp : 28 + 4 * comp, :] = ref[:, CS - 1, :]
    copies = [pltpu.make_async_copy(held, own_ref, out_sems.at[0])]
    for d in range(edges_ref.shape[0]):
        copies.append(pltpu.make_async_copy(held, edges_ref.at[d], out_sems.at[d + 1]))
    for copy in copies:
        copy.start()
    for copy in copies:
        copy.wait()


def take_edges(wind_u, wind_v, token, owners):
    return pl.pallas_call(
        edge_kernel,
        out_shape=(pltpu.HBM((owners, 32, CS), F32), pltpu.HBM((32, CS), F32)),
        in_specs=[hbm(), hbm(), vmem()],
        out_specs=(hbm(), hbm()),
        scratch_shapes=[
            pltpu.VMEM((4, CS, CS), F32),
            pltpu.VMEM((4, CS, CS), F32),
            pltpu.VMEM((32, CS), F32),
            pltpu.SemaphoreType.DMA((8,)),
            pltpu.SemaphoreType.DMA((owners + 1,)),
        ],
        compiler_params=params(4),
        cost_estimate=cost(1000, 4 << 20),
        name="edges",
    )(in_hbm(wind_u), in_hbm(wind_v), token)


def stencil_kernel(u_ref, v_ref, lift_ref, step_x_ref, step_y_ref, coriolis_ref, tend_ref, scale_ref):
    lane = lax.broadcasted_iota(jnp.int32, (CHUNK, CS), 1)
    inner_left, inner_right = lane > 0, lane < CS - 1
    chunks = CS // CHUNK

    def stencil(c, carry):
        r0 = pl.multiple_of(c * CHUNK, CHUNK)
        before = pl.multiple_of(jnp.maximum(r0 - 8, 0), 8)
        after = pl.multiple_of(jnp.minimum(r0 + CHUNK, CS - 8), 8)
        rows = pl.ds(r0, CHUNK)
        half_x = 0.5 / step_x_ref[rows, :]
        half_y = 0.5 / step_y_ref[rows, :]
        rotation = coriolis_ref[rows, :]

        def ends(ref, level):
            top = jnp.where(c == 0, 0.0, ref[level, pl.ds(before, 8), :][7:8])
            bottom = jnp.where(c == chunks - 1, 0.0, ref[level, pl.ds(after, 8), :][0:1])
            return top, bottom

        def rise(mid, top, bottom):
            return jnp.concatenate([mid[1:], bottom], axis=0) - jnp.concatenate(
                [top, mid[: CHUNK - 1]], axis=0
            )

        def across(mid):
            return jnp.where(inner_right, pltpu.roll(mid, CS - 1, 1), 0.0) - jnp.where(
                inner_left, pltpu.roll(mid, 1, 1), 0.0
            )

        def energy(a, b):
            return 0.5 * (a * a + b * b)

        for level in range(4):
            u, v = u_ref[level, rows, :], v_ref[level, rows, :]
            top_u, bottom_u = ends(u_ref, level)
            top_v, bottom_v = ends(v_ref, level)
            kinetic = energy(u, v)
            vort = across(v) * half_x - rise(u, top_u, bottom_u) * half_y + rotation
            slope_x = across(kinetic) * half_x
            slope_y = rise(kinetic, energy(top_u, top_v), energy(bottom_u, bottom_v)) * half_y
            lift = lift_ref[level, rows, :] * 0.5
            if level == 0:
                shear_u, shear_v = u_ref[1, rows, :], v_ref[1, rows, :]
            elif level == 3:
                shear_u, shear_v = -u_ref[2, rows, :], -v_ref[2, rows, :]
            else:
                shear_u = u_ref[level + 1, rows, :] - u_ref[level - 1, rows, :]
                shear_v = v_ref[level + 1, rows, :] - v_ref[level - 1, rows, :]
            tend_ref[0, level, rows, :] = vort * v - slope_x - lift * shear_u
            tend_ref[1, level, rows, :] = -vort * u - slope_y - lift * shear_v
        return carry

    lax.fori_loop(0, chunks, stencil, 0)
    side = lax.broadcasted_iota(jnp.int32, (CS, LANES), 1)
    columns = jnp.where(side == 0, step_x_ref[:, 0:1], step_x_ref[:, CS - 1 : CS])
    steps = jnp.concatenate(
        [
            jnp.transpose(columns)[0:2],
            step_y_ref[0:1, :],
            step_y_ref[CS - 1 : CS, :],
            jnp.ones((4, CS), F32),
        ],
        axis=0,
    )
    scale_ref[...] = 0.5 / steps


def inner_tendencies(*fields):
    return pl.pallas_call(
        stencil_kernel,
        out_shape=(pltpu.HBM((2, 4, CS, CS), F32), pltpu.HBM((8, CS), F32)),
        in_specs=[vmem()] * 6,
        out_specs=(vmem(), vmem()),
        compiler_params=params(10),
        cost_estimate=cost(30 << 20, 6 << 20),
        name="stencil",
    )(*fields)


def remap_kernel(
    target_ref,
    inner_hbm,
    lift_hbm,
    below_hbm,
    above_hbm,
    weights_hbm,
    tend_hbm,
    part_hbm,
    line_hbm,
    weights_ref,
    tend_ref,
    lift_ref,
    below_ref,
    above_ref,
    part_ref,
    line_ref,
    blocks,
    *rest,
):
    accs, (sems, out_sems) = rest[:ACCS], rest[ACCS:]
    block_count = weights_ref.shape[0]
    steps = block_count // GROUP
    lines = GROUP // 2

    def loads(c):
        part = pl.ds(c * GROUP, GROUP)
        rows = pl.ds(pl.multiple_of(c * lines, lines), lines)
        pairs = [
            (inner_hbm.at[:, :, rows], tend_ref.at[:, :, rows]),
            (lift_hbm.at[0, rows], lift_ref.at[0, rows]),
            (lift_hbm.at[3, rows], lift_ref.at[1, rows]),
            (below_hbm.at[:, rows], below_ref.at[:, rows]),
            (above_hbm.at[:, rows], above_ref.at[:, rows]),
            (weights_hbm.at[part], weights_ref.at[part]),
        ]
        return [
            pltpu.make_async_copy(source, dest, sems.at[k, c])
            for k, (source, dest) in enumerate(pairs)
        ]

    def tend_out(c):
        rows = pl.ds(pl.multiple_of(c * lines, lines), lines)
        return pltpu.make_async_copy(
            tend_ref.at[:, :, rows], tend_hbm.at[:, :, rows], sems.at[6, c]
        )

    for c in range(AHEAD):
        for load in loads(c):
            load.start()
    for acc in accs:
        acc[...] = jnp.zeros_like(acc)

    def levels(r0):
        rows = pl.ds(r0, 8)
        for comp in (0, 1):
            for level in range(4):
                value = tend_ref[comp, level, rows, :]
                if level == 0:
                    value = value + lift_ref[0, rows, :] * 0.5 * below_ref[comp, rows, :]
                if level == 3:
                    value = value - lift_ref[1, rows, :] * 0.5 * above_ref[comp, rows, :]
                if level in (0, 3):
                    tend_ref[comp, level, rows, :] = value
                for h in (0, 1):
                    start = r0 * 16 + 8 * h + comp * 4 + level
                    blocks[pl.ds(start, 8, stride=16), :] = value[:, LANES * h : LANES * h + LANES]

    row = lax.broadcasted_iota(jnp.int32, (8, LANES), 0)
    lane = lax.broadcasted_iota(jnp.int32, (8, LANES), 1)
    ones = jnp.where(row == 0, 1.0, 0.0)
    extra = [jnp.where((row == 1) & (lane == q), 1.0, ones) for q in (0, LANES - 1)]

    def remap(c, carry):
        for load in loads(c):
            load.wait()

        @pl.when(c + AHEAD < steps)
        def _():
            for load in loads(c + AHEAD):
                load.start()

        for k in range(lines // 8):
            levels(pl.multiple_of(c * lines + 8 * k, 8))
        tend_out(c).start()
        parts, targets = [], []
        for k in range(GROUP):
            b = c * GROUP + k
            x = blocks[pl.ds(pl.multiple_of(b * 8, 8), 8), :]
            x = jnp.concatenate([x, extra[k & 1]], axis=0).astype(BF16)
            tiles = jnp.concatenate([weights_ref[b, 0], weights_ref[b, 1]], axis=1)
            product = jnp.dot(x, tiles, preferred_element_type=F32)
            for t in (0, 1):
                half = product[:, LANES * t : LANES * t + LANES]
                parts.append(half)
                targets.append(target_ref[t, b])
                line_ref[pl.ds(t * block_count + b, 1), :] = half[9:10]
        for first in range(0, len(parts), ACCS):
            here = range(first, first + ACCS)
            olds = [accs[i - first][targets[i]] for i in here]
            for i, old in zip(here, olds):
                accs[i - first][targets[i]] = old + parts[i]
        return carry

    lax.fori_loop(0, steps, remap, 0)
    line_out = pltpu.make_async_copy(line_ref, line_hbm, out_sems.at[0])
    line_out.start()

    def gather(o, carry):
        sums = []
        for w in range(WINDOWS):
            total = accs[0][o * WINDOWS + w]
            for acc in accs[1:]:
                total = total + acc[o * WINDOWS + w]
            part_ref[o, w * 8 : w * 8 + 8, :] = total[0:8]
            sums.append(total[8:9])
        part_ref[o, 32:40, :] = jnp.concatenate(sums + [jnp.zeros((4, LANES), F32)], axis=0)
        return carry

    lax.fori_loop(0, part_ref.shape[0], gather, 0)
    part_out = pltpu.make_async_copy(part_ref, part_hbm, out_sems.at[1])
    part_out.start()
    for out in (line_out, part_out):
        out.wait()

    def drain(c, carry):
        tend_out(c).wait()
        return carry

    lax.fori_loop(0, steps, drain, 0)


def remap_inner(target, inner, lift, below, above, weights, owners):
    blocks = weights.shape[0]
    return pl.pallas_call(
        remap_kernel,
        out_shape=(
            pltpu.HBM((2, 4, CS, CS), F32),
            pltpu.HBM((owners, 40, LANES), F32),
            pltpu.HBM((2 * blocks, LANES), F32),
        ),
        in_specs=[smem()] + [hbm()] * 5,
        out_specs=(hbm(), hbm(), hbm()),
        scratch_shapes=[
            pltpu.VMEM(weights.shape, BF16),
            pltpu.VMEM((2, 4, CS, CS), F32),
            pltpu.VMEM((2, CS, CS), F32),
            pltpu.VMEM((2, CS, CS), F32),
            pltpu.VMEM((2, CS, CS), F32),
            pltpu.VMEM((owners, 40, LANES), F32),
            pltpu.VMEM((2 * blocks, LANES), F32),
            pltpu.VMEM((blocks * 8, LANES), F32),
        ]
        + [pltpu.VMEM((owners * WINDOWS, 16, LANES), F32)] * ACCS
        + [
            pltpu.SemaphoreType.DMA((7, blocks // GROUP)),
            pltpu.SemaphoreType.DMA((2,)),
        ],
        compiler_params=params(48),
        cost_estimate=cost(2 * 1024 * 16 * 128 * 128, 36 << 20),
        name="remap",
    )(target, *[in_hbm(x) for x in (inner, lift, below, above, weights)])


def reverse_lanes(x):
    rows = x.shape[0]
    i = lax.broadcasted_iota(jnp.int32, (CS, CS), 0)
    j = lax.broadcasted_iota(jnp.int32, (CS, CS), 1)
    flip = jnp.where(i + j == CS - 1, 1.0, 0.0).astype(BF16)
    high = x.astype(BF16)
    rest = x - high.astype(F32)
    mid = rest.astype(BF16)
    low = (rest - mid.astype(F32)).astype(BF16)
    parts = jnp.dot(jnp.concatenate([high, mid, low], axis=0), flip, preferred_element_type=F32)
    return parts[0:rows] + parts[rows : 2 * rows] + parts[2 * rows : 3 * rows]


def fix_kernel(
    source_ref,
    turns_ref,
    target_ref,
    lanes_ref,
    own_ref,
    scale_ref,
    part_hbm,
    line_hbm,
    edges_ref,
    weights_hbm,
    send_hbm,
    delta_ref,
    got,
    ends,
    line_ref,
    send_ref,
    sems,
):
    copies = []
    for s in range(4):
        e = source_ref[0, s]
        copies.append(
            pltpu.make_async_copy(
                edges_ref.at[e >> 2, pl.ds(pl.multiple_of((e & 3) * 8, 8), 8)],
                got.at[s],
                sems.at[s],
            )
        )
    block_count = weights_hbm.shape[0]
    for k, at in enumerate((0, block_count - 2)):
        copies.append(
            pltpu.make_async_copy(
                weights_hbm.at[pl.ds(at, 2)], ends.at[pl.ds(2 * k, 2)], sems.at[4 + k]
            )
        )
    copies.append(pltpu.make_async_copy(line_hbm, line_ref, sems.at[6]))
    copies.append(pltpu.make_async_copy(part_hbm, send_ref, sems.at[7]))
    for copy in copies:
        copy.start()
    for copy in copies:
        copy.wait()

    upper = lax.broadcasted_iota(jnp.int32, (8, CS), 0) < 4
    sign = jnp.where(upper, -1.0, 1.0)
    turned = []
    for s in range(4):
        k = turns_ref[0, s]
        cosine = jnp.where(k == 0, 1.0, 0.0) - jnp.where(k == 2, 1.0, 0.0)
        sine = jnp.where(k == 1, 1.0, 0.0) - jnp.where(k == 3, 1.0, 0.0)
        edge = got[s]
        turned.append(cosine * edge + sine * (sign * pltpu.roll(edge, 4, 0)))
    flipped = reverse_lanes(jnp.concatenate(turned, axis=0))
    deltas = []
    for s in range(4):
        odd = (turns_ref[0, s] & 1) == 1
        halo = jnp.where(odd, flipped[8 * s : 8 * s + 8], turned[s])
        other = pltpu.roll(halo, 4, 0)
        energy = 0.5 * (halo * halo + other * other)
        out = -1.0 if s in (0, 3) else 1.0
        half = scale_ref[s : s + 1, :]
        if s < 2:
            vort = out * half * jnp.where(upper, other, halo)
            kinetic = jnp.where(upper, -out * half * energy, 0.0)
        else:
            vort = out * half * jnp.where(upper, halo, other)
            kinetic = jnp.where(upper, 0.0, out * half * energy)
        across = pltpu.roll(own_ref[8 * s : 8 * s + 8, :], 4, 0)
        delta = kinetic - sign * vort * across
        deltas.append(delta)
        delta_ref[s] = delta

    cell = lax.broadcasted_iota(jnp.int32, (CS, block_count), 0)
    block = lax.broadcasted_iota(jnp.int32, (CS, block_count), 1)
    values = sum(
        jnp.dot(
            deltas[s].astype(BF16),
            jnp.where(block == 2 * cell + s, 1.0, 0.0).astype(BF16),
            preferred_element_type=F32,
        )
        for s in (0, 1)
    )
    values = jnp.concatenate([values, values], axis=1)
    lines = line_ref[...].astype(BF16)
    targets = jnp.broadcast_to(lanes_ref[...], values.shape)
    owners = send_ref.shape[0]
    wide = 4
    for o in range(0, owners, wide):
        rows = [
            jnp.where(targets == w, values, 0.0)
            for w in range(o * WINDOWS, (o + wide) * WINDOWS)
        ]
        columns = jnp.dot(
            jnp.concatenate(rows, axis=0).astype(BF16), lines, preferred_element_type=F32
        )
        for k in range(wide):
            send_ref[o + k, 0:32, :] += columns[32 * k : 32 * k + 32]

    blank = jnp.zeros((8, LANES), F32)
    products = []
    for k in range(4):
        line = deltas[2 + k // 2][:, LANES * (k & 1) : LANES * (k & 1) + LANES]
        x = jnp.concatenate([line, blank], axis=0).astype(BF16)
        tiles = jnp.concatenate([ends[k, 0], ends[k, 1]], axis=1)
        products.append(jnp.dot(x, tiles, preferred_element_type=F32))
    for k, b in enumerate((0, 1, block_count - 2, block_count - 1)):
        for t in (0, 1):
            at = target_ref[t, b]
            rows = pl.ds(pl.multiple_of((at & 3) * 8, 8), 8)
            send_ref[at >> 2, rows, :] += products[k][0:8, LANES * t : LANES * t + LANES]
    out = pltpu.make_async_copy(send_ref, send_hbm, sems.at[8])
    out.start()
    out.wait()


def fix_edges(source, turns, target, lanes, own, scale, part, line, edges, weights):
    return pl.pallas_call(
        fix_kernel,
        out_shape=(pltpu.HBM(part.shape, F32), jax.ShapeDtypeStruct((4, 8, CS), F32)),
        in_specs=[smem()] * 3 + [vmem()] * 3 + [hbm()] * 4,
        out_specs=(hbm(), vmem()),
        scratch_shapes=[
            pltpu.VMEM((4, 8, CS), F32),
            pltpu.VMEM((4, 2, LANES, LANES), BF16),
            pltpu.VMEM(line.shape, F32),
            pltpu.VMEM(part.shape, F32),
            pltpu.SemaphoreType.DMA((9,)),
        ],
        compiler_params=params(10),
        cost_estimate=cost(2 * 1024 * 1024 * 128, 3 << 20),
        name="edge_fix",
    )(source, turns, target, lanes, own, scale, *[in_hbm(x) for x in (part, line, edges, weights)])


def place_kernel(tend_ref, delta_ref, out_ref, cols):
    cols[...] = jnp.transpose(
        jnp.concatenate(
            [delta_ref[0], delta_ref[1], jnp.zeros((LANES - 16, CS), F32)], axis=0
        )
    )
    lane = lax.broadcasted_iota(jnp.int32, (CS, LANES), 1)
    for comp in (0, 1):
        for level in range(4):
            r = comp * 4 + level
            left, right = cols[:, r : r + 1], cols[:, 8 + r : 9 + r]
            value = tend_ref[comp, level, :, 0:LANES]
            out_ref[comp, level, :, 0:LANES] = value + jnp.where(lane == 0, left, 0.0)
            value = tend_ref[comp, level, :, LANES:CS]
            out_ref[comp, level, :, LANES:CS] = value + jnp.where(lane == LANES - 1, right, 0.0)
            out_ref[comp, level, 0:1, :] += delta_ref[2, r : r + 1, :]
            out_ref[comp, level, CS - 1 : CS, :] += delta_ref[3, r : r + 1, :]


def place(tend, delta):
    return pl.pallas_call(
        place_kernel,
        out_shape=jax.ShapeDtypeStruct(tend.shape, F32),
        in_specs=[vmem(), vmem()],
        out_specs=vmem(),
        scratch_shapes=[pltpu.VMEM((CS, LANES), F32)],
        compiler_params=params(8),
        cost_estimate=cost(1 << 20, 4 << 20),
        name="place",
    )(tend, delta)


def finish_kernel(got_ref, out_ref):
    total = got_ref[0]
    for d in range(1, got_ref.shape[0]):
        total = total + got_ref[d]
    for w in range(WINDOWS):
        share = total[8 * w : 8 * w + 8] / jnp.maximum(total[32 + w : 33 + w], 1.0)
        out_ref[0, :, LANES * w : LANES * w + LANES] = share[0:4]
        out_ref[1, :, LANES * w : LANES * w + LANES] = share[4:8]


def finish(got):
    return pl.pallas_call(
        finish_kernel,
        out_shape=jax.ShapeDtypeStruct((2, 4, WINDOWS * LANES), F32),
        in_specs=[vmem()],
        out_specs=vmem(),
        compiler_params=params(4),
        cost_estimate=cost(1000, 1 << 20),
        name="finish",
    )(got)


def per_device(
    wind_u,
    wind_v,
    vertical,
    spacing_x,
    spacing_y,
    coriolis,
    edge_source,
    edge_turns,
    route_owner,
    route_window,
    remap_weights,
):
    owners = lax.axis_size("sub")
    groups = lax.axis_size("lev")
    top, bottom, token = take_levels(wind_u, wind_v)
    edges, own = take_edges(wind_u, wind_v, token, owners)
    below = lax.ppermute(top, "lev", [(i, i + 1) for i in range(groups - 1)])
    above = lax.ppermute(bottom, "lev", [(i + 1, i) for i in range(groups - 1)])
    edges = lax.all_to_all(edges, "sub", split_axis=0, concat_axis=0, tiled=True)
    target = (route_owner * WINDOWS + route_window).T
    lanes = target.reshape(1, target.size)
    inner, scale = inner_tendencies(wind_u, wind_v, vertical, spacing_x, spacing_y, coriolis)
    tend, part, line = remap_inner(target, inner, vertical, below, above, remap_weights, owners)
    send, delta = fix_edges(
        edge_source, edge_turns, target, lanes, own, scale, part, line, edges, remap_weights
    )
    got = lax.all_to_all(send, "sub", split_axis=0, concat_axis=0, tiled=True)
    return place(tend, delta), finish(got)


def solution(mesh):
    placed = (
        P("lev", "sub", None),
        P("lev", "sub", None),
        P("lev", "sub", None),
        P("sub", None),
        P("sub", None),
        P("sub", None),
        P("sub", None),
        P("sub", None),
        P("sub", None),
        P("sub", None),
        P("sub", None, None, None),
    )
    return jax.shard_map(
        per_device,
        mesh=mesh,
        in_specs=placed,
        out_specs=(P(None, "lev", "sub", None), P(None, "lev", "sub")),
        check_vma=False,
    )
```

time: 362 us -> 75.5 us (0.21)
  the two profiles are of different devices: /device:TPU:0 before, /device:TPU:1 now
where the time goes in v1:
time: 75.5 us; the launch traced here: 75 us
  Pallas kernels  32.1 us (43%)
  starting transfers between devices  23 us (30%)
  waiting for transfers between devices  16.3 us (22%)
  local copies, waits for them, and re-layouts  2.76 us (4%)
  between operations  0.88 us (1%)
    pallas_call x1, Pallas kernels, remap_inner(): pl.pallas_call(remap_kernel, out_shape=(pltpu.HBM((2, 4, CS, CS), F32), p...  15.9 us
    all_to_all x1, starting transfers between devices, per_device(): lax.all_to_all(edges, 'sub', split_axis=0, concat_axis=0, tiled=True)  9.87 us
    all_to_all x1, waiting for transfers between devices, per_device(): got = lax.all_to_all(send, 'sub', split_axis=0, concat_axis=0, tiled=True)  7.56 us
    all_to_all x1, starting transfers between devices, per_device(): got = lax.all_to_all(send, 'sub', split_axis=0, concat_axis=0, tiled=True)  5.86 us
    ppermute x1, starting transfers between devices, per_device(): below = lax.ppermute(top, 'lev', [(i, i + 1) for i in range(groups - 1)])  5.37 us
    ppermute x1, waiting for transfers between devices, per_device(): below = lax.ppermute(top, 'lev', [(i, i + 1) for i in range(groups - 1)])  4.83 us
    pallas_call x1, Pallas kernels, fix_edges(): pl.pallas_call(fix_kernel, out_shape=(pltpu.HBM(part.shape, F32), jax.Sha...  4.07 us
    ppermute x1, waiting for transfers between devices, per_device(): above = lax.ppermute(bottom, 'lev', [(i + 1, i) for i in range(groups - 1)])  3.91 us
  transfers between devices with their start and end apart: 4, of which 3 were waited for; matrix products, arithmetic and copies ran while one was open for 0% of the time, Pallas kernels for 29%

profile of v1, /device:TPU:1, one launch (start us, length us, event | category | flops | bytes accessed | tf_op | source)
XLA Modules:
  0.0 75.0 jit_solution(12415335157353385778)
XLA Ops:
  0.6 2.1 %outer_levels.1 = (f32[2,256,256]{2,1,0:T(8,128)}, f32[2,256,256]{2,1,0:T(8,128)}, f32[8,128]{1,0:T(8,128)S(1)}) custom-call(f32[4,256,256]{2,1,0:T(8,128)} %wind_u.3, f32[4,256,256]{2,1,0:T(8,128)} %wind_v.3), custom_call_target="tpu_custom_call" | custom-call | flops 1000 | bytes 2097152 | tf_op jit(solution)/shard_map/outer_levels/pallas_call | solution.py:64
  2.8 0.0 copy-start.13
  2.8 0.0 copy-start.14
  2.8 0.0 copy-start
  2.8 0.0 copy-start.1
  2.8 0.0 copy-start.2
  2.8 0.0 copy-start.4
  2.8 3.6 %edges.1 = (f32[32,32,256]{2,1,0:T(8,128)}, f32[32,256]{1,0:T(8,128)}) custom-call(f32[4,256,256]{2,1,0:T(8,128)} %wind_u.3, f32[4,256,256]{2,1,0:T(8,128)} %wind_v.3, f32[8,128]{1,0:T(8,128)S(1)} %get-tuple-element.18.token_ref), custom_call_target="tpu_custom_call" | custom-call | flops 1000 | bytes 4194304 | tf_op jit(solution)/shard_map/edges/pallas_call | solution.py:116
  6.4 9.9 %all-to-all-start = ((f32[32,32,256]{2,1,0:T(8,128)}), f32[32,32,256]{2,1,0:T(8,128)}, u32[]{:S(2)}, u32[]{:S(2)}) async-start(f32[32,32,256]{2,1,0:T(8,128)} %get-tuple-element.23), calls=%async_computation | async-start | bytes 2097152 | tf_op jit(solution)/shard_map/all_to_all | solution.py:597
  16.3 5.4 %collective-permute-start = (f32[2,256,256]{2,1,0:T(8,128)}, f32[2,256,256]{2,1,0:T(8,128)S(1)}, u32[]{:S(2)}, u32[]{:S(2)}) collective-permute-start(f32[2,256,256]{2,1,0:T(8,128)} %get-tuple-element.15), channel_id=1, source_target_pairs={{0,1},{1,2},{2,3},{4,5},{5,6},{6,7},{8,9},{9,10},{10,11},{12,13},{... | collective-permute-start | bytes 1572872 | tf_op jit(solution)/shard_map/ppermute | solution.py:595
  21.7 1.9 %collective-permute-start.1 = (f32[2,256,256]{2,1,0:T(8,128)}, f32[2,256,256]{2,1,0:T(8,128)S(1)}, u32[]{:S(2)}, u32[]{:S(2)}) collective-permute-start(f32[2,256,256]{2,1,0:T(8,128)} %get-tuple-element.16), channel_id=1, source_target_pairs={{1,0},{2,1},{3,2},{5,4},{6,5},{7,6},{9,8},{10,9},{11,10},{13,12},{... | collective-permute-start | bytes 1572872 | tf_op jit(solution)/shard_map/ppermute | solution.py:596
  23.6 0.0 copy-done.13
  23.6 0.0 copy-done.14
  23.6 0.0 copy-done
  23.6 0.0 copy-done.1
  23.7 0.0 copy-done.2
  23.7 0.0 copy-done.4
  23.7 0.0 copy-start.5
  23.7 0.9 %copy-done.5 = f32[256,256]{1,0:T(8,128)S(1)} copy-done((f32[256,256]{1,0:T(8,128)S(1)}, f32[256,256]{1,0:T(8,128)}, u32[]{:S(2)}) %copy-start.5) | copy-done | bytes 262168
  24.6 0.9 %copy-done.6 = f32[256,256]{1,0:T(8,128)S(1)} copy-done((f32[256,256]{1,0:T(8,128)S(1)}, f32[256,256]{1,0:T(8,128)}, u32[]{:S(2)}) %copy-start.6) | copy-done | bytes 262168
  25.6 3.7 %stencil.1 = (f32[2,4,256,256]{3,2,1,0:T(8,128)}, f32[8,256]{1,0:T(8,128)}) custom-call(f32[4,256,256]{2,1,0:T(8,128)S(1)} %copy-done, f32[4,256,256]{2,1,0:T(8,128)S(1)} %copy-done.1, f32[4,256,256]{2,1,0:T(8,128)S(1)} %copy-done.2, f32[256,256]{1,0:T(8,128)S(1)} %copy-done.4, f32[256,256]{1,0:T(8,128)S(1)} %copy-done.5, f32[256,256]{1,0:T(8,128)S(1)} %copy-done.6), custom_call_target="tpu_custom_call" | custom-call | flops 31457280 | bytes 6291456 | tf_op jit(solution)/shard_map/stencil/pallas_call | solution.py:202
  29.2 4.8 %collective-permute-done.below_hbm = f32[2,256,256]{2,1,0:T(8,128)S(1)} collective-permute-done((f32[2,256,256]{2,1,0:T(8,128)}, f32[2,256,256]{2,1,0:T(8,128)S(1)}, u32[]{:S(2)}, u32[]{:S(2)}) %collective-permute-start) | collective-permute-done | bytes 524320 | tf_op jit(solution)/shard_map/ppermute | solution.py:595
  34.1 3.9 %collective-permute-done.1.above_hbm = f32[2,256,256]{2,1,0:T(8,128)S(1)} collective-permute-done((f32[2,256,256]{2,1,0:T(8,128)}, f32[2,256,256]{2,1,0:T(8,128)S(1)}, u32[]{:S(2)}, u32[]{:S(2)}) %collective-permute-start.1) | collective-permute-done | bytes 524320 | tf_op jit(solution)/shard_map/ppermute | solution.py:596
  38.0 0.0 copy-done.11
  38.0 0.8 %copy-done.12 = f32[2,256,256]{2,1,0:T(8,128)} copy-done((f32[2,256,256]{2,1,0:T(8,128)}, f32[2,256,256]{2,1,0:T(8,128)S(1)}, u32[]{:S(2)}) %copy-start.12) | copy-done | bytes 524312
  38.8 15.9 %remap.1 = (f32[2,4,256,256]{3,2,1,0:T(8,128)}, f32[32,40,128]{2,1,0:T(8,128)}, f32[1024,128]{1,0:T(8,128)}) custom-call(s32[2,512]{1,0:T(2,128)S(1)} %get-tuple-element.27.target_ref, f32[2,4,256,256]{3,2,1,0:T(8,128)} %get-tuple-element.14.inner_hbm, f32[4,256,256]{2,1,0:T(8,128)} %lift_hbm.1, f32[2,256,256]{2,1,0:T(8,128)} %copy-done.11, ...), custom_call_target="tpu_custom_call" | custom-call | flops 536870912 | bytes 37748736 | tf_op jit(solution)/shard_map/remap/pallas_call | solution.py:347
  54.7 0.0 all-to-all-done.edges_ref
  54.8 4.1 %edge_fix.1 = (f32[32,40,128]{2,1,0:T(8,128)}, f32[4,8,256]{2,1,0:T(8,128)S(1)}) custom-call(s32[1,4]{1,0:T(1,128)S(1)} %copy-done.9, s32[1,4]{1,0:T(1,128)S(1)} %copy-done.10, s32[2,512]{1,0:T(2,128)S(1)} %get-tuple-element.27.target_ref, s32[1,1024]{1,0:T(1,128)S(1)} %bitcast.6, f32[32,256]{1,0:T(8,128)S(1)} %copy-done.7, f32[8,256]{1,0:T(8,128)S(1)} %copy-done.8, ...), custom_call_target="tpu_custom_call" | custom-call | flops 268435456 | bytes 3145728 | tf_op jit(solution)/shard_map/edge_fix/pallas_call | solution.py:506
  58.9 5.9 %all-to-all-start.1 = ((f32[32,40,128]{2,1,0:T(8,128)}), f32[32,40,128]{2,1,0:T(8,128)S(1)}, u32[]{:S(2)}, u32[]{:S(2)}) async-start(f32[32,40,128]{2,1,0:T(8,128)} %get-tuple-element.25), calls=%async_computation.1 | async-start | bytes 1310720 | tf_op jit(solution)/shard_map/all_to_all | solution.py:605
  64.7 2.1 %place.1 = f32[2,4,256,256]{3,2,1,0:T(8,128)} custom-call(f32[2,4,256,256]{3,2,1,0:T(8,128)S(1)} %copy-done.3, f32[4,8,256]{2,1,0:T(8,128)S(1)} %get-tuple-element.24.delta_ref), custom_call_target="tpu_custom_call" | custom-call | flops 1048576 | bytes 4194304 | tf_op jit(solution)/shard_map/place/pallas_call | solution.py:544
  66.8 7.6 %all-to-all-done.1.got_ref = f32[32,40,128]{2,1,0:T(8,128)S(1)} async-done(((f32[32,40,128]{2,1,0:T(8,128)}), f32[32,40,128]{2,1,0:T(8,128)S(1)}, u32[]{:S(2)}, u32[]{:S(2)}) %all-to-all-start.1) | async-done | bytes 655392 | tf_op jit(solution)/shard_map/all_to_all | solution.py:605
  74.4 0.7 finish.1
  (15 shorter events, 0.0 us)
Async XLA Ops:
  2.8 20.8 %copy-start.13 = (s32[512,2]{0,1:T(2,128)S(1)}, s32[512,2]{0,1:T(2,128)}, u32[]{:S(2)}) copy-start(s32[512,2]{0,1:T(2,128)} %param.20) | copy-start | bytes 12292
  2.8 20.8 %copy-start.14 = (s32[512,2]{0,1:T(2,128)S(1)}, s32[512,2]{0,1:T(2,128)}, u32[]{:S(2)}) copy-start(s32[512,2]{0,1:T(2,128)} %param.19) | copy-start | bytes 12292
  2.8 20.9 %copy-start = (f32[4,256,256]{2,1,0:T(8,128)S(1)}, f32[4,256,256]{2,1,0:T(8,128)}, u32[]{:S(2)}) copy-start(f32[4,256,256]{2,1,0:T(8,128)} %wind_u.3) | copy-start | bytes 3145732
  2.8 20.9 %copy-start.1 = (f32[4,256,256]{2,1,0:T(8,128)S(1)}, f32[4,256,256]{2,1,0:T(8,128)}, u32[]{:S(2)}) copy-start(f32[4,256,256]{2,1,0:T(8,128)} %wind_v.3) | copy-start | bytes 3145732
  2.8 20.9 %copy-start.2 = (f32[4,256,256]{2,1,0:T(8,128)S(1)}, f32[4,256,256]{2,1,0:T(8,128)}, u32[]{:S(2)}) copy-start(f32[4,256,256]{2,1,0:T(8,128)} %lift_hbm.1) | copy-start | bytes 3145732
  2.8 20.9 %copy-start.4 = (f32[256,256]{1,0:T(8,128)S(1)}, f32[256,256]{1,0:T(8,128)}, u32[]{:S(2)}) copy-start(f32[256,256]{1,0:T(8,128)} %step_x_ref.1) | copy-start | bytes 786436
  6.4 48.3 %all-to-all-start = ((f32[32,32,256]{2,1,0:T(8,128)}), f32[32,32,256]{2,1,0:T(8,128)}, u32[]{:S(2)}, u32[]{:S(2)}) async-start(f32[32,32,256]{2,1,0:T(8,128)} %get-tuple-element.23), calls=%async_computation | async-start | bytes 2097152 | tf_op jit(solution)/shard_map/all_to_all | solution.py:597
  16.3 17.8 %collective-permute-start = (f32[2,256,256]{2,1,0:T(8,128)}, f32[2,256,256]{2,1,0:T(8,128)S(1)}, u32[]{:S(2)}, u32[]{:S(2)}) collective-permute-start(f32[2,256,256]{2,1,0:T(8,128)} %get-tuple-element.15), channel_id=1, source_target_pairs={{0,1},{1,2},{2,3},{4,5},{5,6},{6,7},{8,9},{9,10},{10,11},{12,13},{... | collective-permute-start | bytes 1572872 | tf_op jit(solution)/shard_map/ppermute | solution.py:595
  21.7 16.3 %collective-permute-start.1 = (f32[2,256,256]{2,1,0:T(8,128)}, f32[2,256,256]{2,1,0:T(8,128)S(1)}, u32[]{:S(2)}, u32[]{:S(2)}) collective-permute-start(f32[2,256,256]{2,1,0:T(8,128)} %get-tuple-element.16), channel_id=1, source_target_pairs={{1,0},{2,1},{3,2},{5,4},{6,5},{7,6},{9,8},{10,9},{11,10},{13,12},{... | collective-permute-start | bytes 1572872 | tf_op jit(solution)/shard_map/ppermute | solution.py:596
  23.7 1.0 %copy-start.5 = (f32[256,256]{1,0:T(8,128)S(1)}, f32[256,256]{1,0:T(8,128)}, u32[]{:S(2)}) copy-start(f32[256,256]{1,0:T(8,128)} %step_y_ref.1) | copy-start | bytes 786436
  24.6 0.9 %copy-start.6 = (f32[256,256]{1,0:T(8,128)S(1)}, f32[256,256]{1,0:T(8,128)}, u32[]{:S(2)}) copy-start(f32[256,256]{1,0:T(8,128)} %coriolis_ref.1) | copy-start | bytes 786436
  34.1 3.9 %copy-start.11 = (f32[2,256,256]{2,1,0:T(8,128)}, f32[2,256,256]{2,1,0:T(8,128)S(1)}, u32[]{:S(2)}) copy-start(f32[2,256,256]{2,1,0:T(8,128)S(1)} %collective-permute-done.below_hbm) | copy-start | bytes 1572868
  38.0 0.8 %copy-start.12 = (f32[2,256,256]{2,1,0:T(8,128)}, f32[2,256,256]{2,1,0:T(8,128)S(1)}, u32[]{:S(2)}) copy-start(f32[2,256,256]{2,1,0:T(8,128)S(1)} %collective-permute-done.1.above_hbm) | copy-start | bytes 1572868
  38.8 16.0 %copy-start.7 = (f32[32,256]{1,0:T(8,128)S(1)}, f32[32,256]{1,0:T(8,128)}, u32[]{:S(2)}) copy-start(f32[32,256]{1,0:T(8,128)} %get-tuple-element.19.own_ref) | copy-start | bytes 98308
  38.8 16.0 %copy-start.8 = (f32[8,256]{1,0:T(8,128)S(1)}, f32[8,256]{1,0:T(8,128)}, u32[]{:S(2)}) copy-start(f32[8,256]{1,0:T(8,128)} %get-tuple-element.20.scale_ref) | copy-start | bytes 24580
  38.8 16.0 %copy-start.9 = (s32[1,4]{1,0:T(1,128)S(1)}, s32[1,4]{1,0:T(1,128)}, u32[]{:S(2)}) copy-start(s32[1,4]{1,0:T(1,128)} %source_ref.1) | copy-start | bytes 52
  38.8 16.0 %copy-start.10 = (s32[1,4]{1,0:T(1,128)S(1)}, s32[1,4]{1,0:T(1,128)}, u32[]{:S(2)}) copy-start(s32[1,4]{1,0:T(1,128)} %turns_ref.1) | copy-start | bytes 52
  54.8 9.9 %copy-start.3 = (f32[2,4,256,256]{3,2,1,0:T(8,128)S(1)}, f32[2,4,256,256]{3,2,1,0:T(8,128)}, u32[]{:S(2)}) copy-start(f32[2,4,256,256]{3,2,1,0:T(8,128)} %get-tuple-element.17.tend_ref) | copy-start | bytes 6291460
  58.9 15.5 %all-to-all-start.1 = ((f32[32,40,128]{2,1,0:T(8,128)}), f32[32,40,128]{2,1,0:T(8,128)S(1)}, u32[]{:S(2)}, u32[]{:S(2)}) async-start(f32[32,40,128]{2,1,0:T(8,128)} %get-tuple-element.25), calls=%async_computation.1 | async-start | bytes 1310720 | tf_op jit(solution)/shard_map/all_to_all | solution.py:605

commit v2 on v1

v2 whole, which is shorter than its diff:
```python
import jax
import jax.numpy as jnp
from jax import lax
from jax.experimental import pallas as pl
from jax.experimental.pallas import tpu as pltpu
from jax.sharding import PartitionSpec as P

WINDOWS = 4
CS = 256
LANES = 128
CHUNK = 16
ACCS = 4
GROUP = 64
PIECE = 32
HELD = 128
SPLIT = CS // CHUNK // 2 - 1
QUARTERS = 4
F32 = jnp.float32
BF16 = jnp.bfloat16


def vmem():
    return pl.BlockSpec(memory_space=pltpu.VMEM)


def smem():
    return pl.BlockSpec(memory_space=pltpu.SMEM)


def anywhere():
    return pl.BlockSpec(memory_space=pl.ANY)


def hbm():
    return pl.BlockSpec(memory_space=pltpu.HBM)


def in_hbm(x):
    return pltpu.with_memory_space_constraint(x, pltpu.HBM)


def in_vmem(x):
    return pltpu.with_memory_space_constraint(x, pltpu.VMEM)


def params(mib):
    return pltpu.CompilerParams(vmem_limit_bytes=mib * 1024 * 1024)


def cost(flops, size):
    return pl.CostEstimate(flops=flops, bytes_accessed=size, transcendentals=0)


def edge_kernel(
    wind_u, wind_v, edges_ref, own_ref, far_ref, near_ref, u_ref, v_ref, held, in_sems, out_sems
):
    loads, sends = [], []
    order = [(comp, level) for level in (0, 3, 1, 2) for comp in (0, 1)]
    winds, refs = (wind_u, wind_v), (u_ref, v_ref)
    for k, (comp, level) in enumerate(order):
        loads.append(
            pltpu.make_async_copy(winds[comp].at[level], refs[comp].at[level], in_sems.at[k])
        )
    for load in loads:
        load.start()
    lane = lax.broadcasted_iota(jnp.int32, (CS, LANES), 1)
    columns = jnp.zeros((CS, LANES), F32)
    for k, (comp, level) in enumerate(order):
        loads[k].wait()
        ref = refs[comp]
        if level in (0, 3):
            if level == 3:
                odd = lax.rem(lax.axis_index("lev"), 2)
                for n, (out, at) in enumerate(((far_ref, 3 * odd), (near_ref, 3 - 3 * odd))):
                    sem = out_sems.at[2 * comp + n]
                    sends.append(pltpu.make_async_copy(ref.at[at], out.at[comp], sem))
                    sends[-1].start()
        for side in (0, 1):
            at = 0 if side == 0 else CS - 1
            column = ref[level, :, pl.ds(at, 1)]
            columns = jnp.where(lane == side * 8 + comp * 4 + level, column, columns)
    parts = [jnp.transpose(columns)[0:16, :]]
    for at in (0, CS - 1):
        for ref in refs:
            parts.append(ref[:, at, :])
    edges = jnp.concatenate(parts, axis=0)
    owners = held.shape[0]
    for d in range(owners):
        held[d] = edges
    sends.append(pltpu.make_async_copy(held.at[0], own_ref, out_sems.at[4]))
    sends[-1].start()
    for k in range(4):
        part = pl.ds(k * (owners // 4), owners // 4)
        sends.append(pltpu.make_async_copy(held.at[part], edges_ref.at[part], out_sems.at[k + 5]))
        sends[-1].start()
    for send in sends:
        send.wait()


def take_edges(wind_u, wind_v, owners):
    return pl.pallas_call(
        edge_kernel,
        out_shape=(
            pltpu.HBM((owners, 32, CS), F32),
            pltpu.HBM((32, CS), F32),
            pltpu.HBM((2, CS, CS), F32),
            pltpu.HBM((2, CS, CS), F32),
        ),
        in_specs=[hbm(), hbm()],
        out_specs=(hbm(),) * 4,
        scratch_shapes=[
            pltpu.VMEM((4, CS, CS), F32),
            pltpu.VMEM((4, CS, CS), F32),
            pltpu.VMEM((owners, 32, CS), F32),
            pltpu.SemaphoreType.DMA((8,)),
            pltpu.SemaphoreType.DMA((9,)),
        ],
        compiler_params=params(5),
        cost_estimate=cost(1000, 4 << 20),
        name="edges",
    )(in_hbm(wind_u), in_hbm(wind_v))


def spread(blocks, r0, r, value):
    for part in range(value.shape[0] // 8):
        for h in (0, 1):
            start = (r0 + part * 8) * 16 + 8 * h + r
            blocks[pl.ds(start, 8, stride=16), :] = value[
                8 * part : 8 * part + 8, LANES * h : LANES * h + LANES
            ]


def half_loads(sources, dests, sems):
    halves = []
    for h in (0, 1):
        rows = pl.ds(h * (CS // 2), CS // 2)
        copies = []
        for k, (source, dest) in enumerate(zip(sources, dests)):
            if len(source.shape) == 3:
                source, dest = source.at[:, rows], dest.at[:, rows]
            else:
                source, dest = source.at[rows], dest.at[rows]
            copies.append(pltpu.make_async_copy(source, dest, sems.at[h, k]))
        halves.append(copies)
    return halves


def stencil_step(u_ref, v_ref, lift_ref, step_x_ref, step_y_ref, coriolis_ref, put):
    lane = lax.broadcasted_iota(jnp.int32, (CHUNK, CS), 1)
    inner_left, inner_right = lane > 0, lane < CS - 1
    chunks = CS // CHUNK

    def stencil(c, carry):
        r0 = pl.multiple_of(c * CHUNK, CHUNK)
        before = pl.multiple_of(jnp.maximum(r0 - 8, 0), 8)
        after = pl.multiple_of(jnp.minimum(r0 + CHUNK, CS - 8), 8)
        rows = pl.ds(r0, CHUNK)
        half_x = 0.5 / step_x_ref[rows, :]
        half_y = 0.5 / step_y_ref[rows, :]
        rotation = coriolis_ref[rows, :]

        def ends(ref, level):
            top = jnp.where(c == 0, 0.0, ref[level, pl.ds(before, 8), :][7:8])
            bottom = jnp.where(c == chunks - 1, 0.0, ref[level, pl.ds(after, 8), :][0:1])
            return top, bottom

        def rise(mid, top, bottom):
            return jnp.concatenate([mid[1:], bottom], axis=0) - jnp.concatenate(
                [top, mid[: CHUNK - 1]], axis=0
            )

        def across(mid):
            return jnp.where(inner_right, pltpu.roll(mid, CS - 1, 1), 0.0) - jnp.where(
                inner_left, pltpu.roll(mid, 1, 1), 0.0
            )

        def energy(a, b):
            return 0.5 * (a * a + b * b)

        for level in range(4):
            u, v = u_ref[level, rows, :], v_ref[level, rows, :]
            top_u, bottom_u = ends(u_ref, level)
            top_v, bottom_v = ends(v_ref, level)
            kinetic = energy(u, v)
            vort = across(v) * half_x - rise(u, top_u, bottom_u) * half_y + rotation
            slope_x = across(kinetic) * half_x
            slope_y = rise(kinetic, energy(top_u, top_v), energy(bottom_u, bottom_v)) * half_y
            lift = lift_ref[level, rows, :] * 0.5
            if level == 0:
                shear_u, shear_v = u_ref[1, rows, :], v_ref[1, rows, :]
            elif level == 3:
                shear_u, shear_v = -u_ref[2, rows, :], -v_ref[2, rows, :]
            else:
                shear_u = u_ref[level + 1, rows, :] - u_ref[level - 1, rows, :]
                shear_v = v_ref[level + 1, rows, :] - v_ref[level - 1, rows, :]
            put(r0, level, vort * v - slope_x - lift * shear_u)
            put(r0, 4 + level, -vort * u - slope_y - lift * shear_v)
        return carry

    return stencil


def stencil_kernel(
    u_hbm,
    v_hbm,
    step_x_hbm,
    step_y_hbm,
    coriolis_hbm,
    lift_hbm,
    weights_hbm,
    blocks,
    scale_ref,
    lift_ref,
    held_ref,
    u_ref,
    v_ref,
    step_x_ref,
    step_y_ref,
    coriolis_ref,
    field_sems,
    sems,
):
    loads = half_loads(
        (u_hbm, v_hbm, step_x_hbm, step_y_hbm, coriolis_hbm, lift_hbm),
        (u_ref, v_ref, step_x_ref, step_y_ref, coriolis_ref, lift_ref),
        field_sems,
    )
    for load in loads[0] + loads[1]:
        load.start()
    copies = []
    for k in range(HELD // PIECE):
        part = pl.ds(k * PIECE, PIECE)
        copies.append(pltpu.make_async_copy(weights_hbm.at[part], held_ref.at[part], sems.at[k]))
    step = stencil_step(
        u_ref, v_ref, lift_ref, step_x_ref, step_y_ref, coriolis_ref, lambda *at: spread(blocks, *at)
    )
    for load in loads[0]:
        load.wait()
    for copy in copies:
        copy.start()
    lax.fori_loop(0, SPLIT, step, 0)
    for load in loads[1]:
        load.wait()
    lax.fori_loop(SPLIT, CS // CHUNK, step, 0)
    side = lax.broadcasted_iota(jnp.int32, (CS, LANES), 1)
    columns = jnp.where(side == 0, step_x_ref[:, 0:1], step_x_ref[:, CS - 1 : CS])
    steps = jnp.concatenate(
        [
            jnp.transpose(columns)[0:2],
            step_y_ref[0:1, :],
            step_y_ref[CS - 1 : CS, :],
            jnp.ones((4, CS), F32),
        ],
        axis=0,
    )
    scale_ref[...] = 0.5 / steps
    for copy in copies:
        copy.wait()


def inner_tendencies(fields, weights):
    return pl.pallas_call(
        stencil_kernel,
        out_shape=(
            pltpu.VMEM((CS * 16, LANES), F32),
            pltpu.HBM((8, CS), F32),
            pltpu.VMEM((4, CS, CS), F32),
            pltpu.VMEM((HELD,) + weights.shape[1:], BF16),
        ),
        in_specs=[hbm()] * 7,
        out_specs=(vmem(),) * 4,
        scratch_shapes=[
            pltpu.VMEM((4, CS, CS), F32),
            pltpu.VMEM((4, CS, CS), F32),
            pltpu.VMEM((CS, CS), F32),
            pltpu.VMEM((CS, CS), F32),
            pltpu.VMEM((CS, CS), F32),
            pltpu.SemaphoreType.DMA((2, 6)),
            pltpu.SemaphoreType.DMA((HELD // PIECE,)),
        ],
        compiler_params=params(10),
        cost_estimate=cost(0, 0),
        name="stencil",
    )(*[in_hbm(x) for x in fields], in_hbm(weights))


def outer_terms(odd, lift_ref, far_ref, near_ref):
    sides = ((far_ref, 3 * odd, odd), (near_ref, 3 - 3 * odd, 1 - odd))

    def terms(rows):
        out = []
        for ref, level, top in sides:
            lift = lift_ref[level, rows, :] * jnp.where(top == 1, -0.5, 0.5)
            out += [(comp, level, lift * ref[comp, rows, :]) for comp in (0, 1)]
        return out

    return terms


def remap_kernel(
    owner_ref,
    window_ref,
    blocks_in,
    held_ref,
    lift_ref,
    far_ref,
    near_ref,
    weights_hbm,
    part_hbm,
    line_hbm,
    far_hbm,
    near_hbm,
    part_ref,
    blocks,
    line_ref,
    rest_ref,
    *rest,
):
    accs, (sems, in_sems) = rest[:ACCS], rest[ACCS:]
    block_count = weights_hbm.shape[0]
    steps = block_count // GROUP
    held_steps = HELD // GROUP
    lines = GROUP // 2

    def load(c):
        source = weights_hbm.at[pl.ds(HELD + c * PIECE, PIECE)]
        return pltpu.make_async_copy(source, rest_ref.at[pl.ds(c * PIECE, PIECE)], sems.at[c])

    for acc in accs:
        acc[...] = jnp.zeros_like(acc)
    for c in range((block_count - HELD) // PIECE):
        load(c).start()
    outs = [
        pltpu.make_async_copy(far_ref, far_hbm, in_sems.at[3]),
        pltpu.make_async_copy(near_ref, near_hbm, in_sems.at[4]),
    ]
    for out in outs:
        out.start()
    odd = lax.rem(lax.axis_index("lev"), 2)
    terms = outer_terms(odd, lift_ref, far_ref, near_ref)

    def levels(r0):
        part = pl.ds(pl.multiple_of(r0 * 16, 128), 128)
        blocks[part, :] = blocks_in[part, :]
        for comp, level, value in terms(pl.ds(r0, 8)):
            for h in (0, 1):
                spot = pl.ds(r0 * 16 + 8 * h + comp * 4 + level, 8, stride=16)
                half = value[:, LANES * h : LANES * h + LANES]
                blocks[spot, :] = blocks_in[spot, :] + half

    row = lax.broadcasted_iota(jnp.int32, (8, LANES), 0)
    lane = lax.broadcasted_iota(jnp.int32, (8, LANES), 1)
    ones = jnp.where(row == 0, 1.0, 0.0)
    extra = [jnp.where((row == 1) & (lane == q), 1.0, ones) for q in (0, LANES - 1)]

    def remap(c, weights_ref, first_block):
        for k in range(lines // 8):
            levels(pl.multiple_of(c * lines + 8 * k, 8))
        parts, targets = [], []
        for k in range(GROUP):
            b = c * GROUP + k
            x = blocks[pl.ds(pl.multiple_of(b * 8, 8), 8), :]
            x = jnp.concatenate([x, extra[k & 1]], axis=0).astype(BF16)
            here = b - first_block
            tiles = jnp.concatenate([weights_ref[here, 0], weights_ref[here, 1]], axis=1)
            product = jnp.dot(x, tiles, preferred_element_type=F32)
            for t in (0, 1):
                half = product[:, LANES * t : LANES * t + LANES]
                parts.append(half)
                targets.append(owner_ref[t, b] * WINDOWS + window_ref[t, b])
                line_ref[pl.ds(t * block_count + b, 1), :] = half[9:10]
        for first in range(0, len(parts), ACCS):
            here = range(first, first + ACCS)
            olds = [accs[i - first][targets[i]] for i in here]
            for i, old in zip(here, olds):
                accs[i - first][targets[i]] = old + parts[i]

    def remap_held(c, carry):
        remap(c, held_ref, 0)
        return carry

    def remap_rest(c, carry):
        for k in range(GROUP // PIECE):
            load((c - held_steps) * (GROUP // PIECE) + k).wait()
        remap(c, rest_ref, HELD)
        return carry

    lax.fori_loop(0, held_steps, remap_held, 0)
    lax.fori_loop(held_steps, steps, remap_rest, 0)
    line_out = pltpu.make_async_copy(line_ref, line_hbm, in_sems.at[2])
    line_out.start()

    def gather(o, carry):
        sums = []
        for w in range(WINDOWS):
            total = accs[0][o * WINDOWS + w]
            for acc in accs[1:]:
                total = total + acc[o * WINDOWS + w]
            part_ref[o, w * 8 : w * 8 + 8, :] = total[0:8]
            sums.append(total[8:9])
        part_ref[o, 32:40, :] = jnp.concatenate(sums + [jnp.zeros((4, LANES), F32)], axis=0)
        return carry

    size = part_ref.shape[0] // QUARTERS
    for k in range(QUARTERS):
        lax.fori_loop(k * size, (k + 1) * size, gather, 0)
        spot = pl.ds(k * size, size)
        outs.append(pltpu.make_async_copy(part_ref.at[spot], part_hbm.at[spot], in_sems.at[5 + k]))
        outs[-1].start()
    for out in outs + [line_out]:
        out.wait()


def remap_inner(route, blocks, held, lift, far, near, weights, owners):
    count = weights.shape[0]
    return pl.pallas_call(
        remap_kernel,
        out_shape=(
            pltpu.HBM((owners, 40, LANES), F32),
            pltpu.HBM((2 * count, LANES), F32),
            pltpu.HBM((2, CS, CS), F32),
            pltpu.HBM((2, CS, CS), F32),
        ),
        in_specs=[smem()] * 2 + [vmem()] * 5 + [hbm()],
        out_specs=(hbm(),) * 4,
        scratch_shapes=[
            pltpu.VMEM((owners, 40, LANES), F32),
            pltpu.VMEM(blocks.shape, F32),
            pltpu.VMEM((2 * count, LANES), F32),
            pltpu.VMEM((count - HELD,) + weights.shape[1:], BF16),
        ]
        + [pltpu.VMEM((owners * WINDOWS, 16, LANES), F32)] * ACCS
        + [
            pltpu.SemaphoreType.DMA(((count - HELD) // PIECE,)),
            pltpu.SemaphoreType.DMA((5 + QUARTERS,)),
        ],
        compiler_params=params(36),
        cost_estimate=cost(10**15, 1 << 40),
        name="remap",
    )(
        *route,
        *[in_vmem(x) for x in (blocks, held, lift)],
        far,
        near,
        in_hbm(weights),
    )


def reverse_lanes(x):
    rows = x.shape[0]
    i = lax.broadcasted_iota(jnp.int32, (CS, CS), 0)
    j = lax.broadcasted_iota(jnp.int32, (CS, CS), 1)
    flip = jnp.where(i + j == CS - 1, 1.0, 0.0).astype(BF16)
    high = x.astype(BF16)
    rest = x - high.astype(F32)
    mid = rest.astype(BF16)
    low = (rest - mid.astype(F32)).astype(BF16)
    parts = jnp.dot(jnp.concatenate([high, mid, low], axis=0), flip, preferred_element_type=F32)
    return parts[0:rows] + parts[rows : 2 * rows] + parts[2 * rows : 3 * rows]


def fix_kernel(
    source_ref,
    turns_ref,
    owner_ref,
    window_ref,
    owners_ref,
    windows_ref,
    own_ref,
    scale_ref,
    edges_any,
    part_hbm,
    line_hbm,
    weights_hbm,
    send_hbm,
    delta_ref,
    got,
    ends,
    line_ref,
    send_ref,
    sems,
):
    edge_copies, copies = [], []
    for s in range(4):
        e = source_ref[0, s]
        spot = edges_any.at[e >> 2, pl.ds(pl.multiple_of((e & 3) * 8, 8), 8)]
        edge_copies.append(pltpu.make_async_copy(spot, got.at[s], sems.at[s]))
    block_count = weights_hbm.shape[0]
    for k, at in enumerate((0, block_count - 2)):
        copies.append(
            pltpu.make_async_copy(
                weights_hbm.at[pl.ds(at, 2)], ends.at[pl.ds(2 * k, 2)], sems.at[4 + k]
            )
        )
    copies.append(pltpu.make_async_copy(line_hbm, line_ref, sems.at[6]))
    copies.append(pltpu.make_async_copy(part_hbm, send_ref, sems.at[7]))
    for copy in edge_copies + copies:
        copy.start()
    for copy in edge_copies:
        copy.wait()

    upper = lax.broadcasted_iota(jnp.int32, (8, CS), 0) < 4
    sign = jnp.where(upper, -1.0, 1.0)
    turned = []
    for s in range(4):
        k = turns_ref[0, s]
        cosine = jnp.where(k == 0, 1.0, 0.0) - jnp.where(k == 2, 1.0, 0.0)
        sine = jnp.where(k == 1, 1.0, 0.0) - jnp.where(k == 3, 1.0, 0.0)
        edge = got[s]
        turned.append(cosine * edge + sine * (sign * pltpu.roll(edge, 4, 0)))
    flipped = reverse_lanes(jnp.concatenate(turned, axis=0))
    deltas = []
    for s in range(4):
        odd = (turns_ref[0, s] & 1) == 1
        halo = jnp.where(odd, flipped[8 * s : 8 * s + 8], turned[s])
        other = pltpu.roll(halo, 4, 0)
        energy = 0.5 * (halo * halo + other * other)
        out = -1.0 if s in (0, 3) else 1.0
        half = scale_ref[s : s + 1, :]
        if s < 2:
            vort = out * half * jnp.where(upper, other, halo)
            kinetic = jnp.where(upper, -out * half * energy, 0.0)
        else:
            vort = out * half * jnp.where(upper, halo, other)
            kinetic = jnp.where(upper, 0.0, out * half * energy)
        across = pltpu.roll(own_ref[8 * s : 8 * s + 8, :], 4, 0)
        delta = kinetic - sign * vort * across
        deltas.append(delta)
        delta_ref[s] = delta

    cell = lax.broadcasted_iota(jnp.int32, (CS, block_count), 0)
    block = lax.broadcasted_iota(jnp.int32, (CS, block_count), 1)
    for copy in copies:
        copy.wait()
    blank = jnp.zeros((8, LANES), F32)
    products = []
    for k in range(4):
        line = deltas[2 + k // 2][:, LANES * (k & 1) : LANES * (k & 1) + LANES]
        x = jnp.concatenate([line, blank], axis=0).astype(BF16)
        tiles = jnp.concatenate([ends[k, 0], ends[k, 1]], axis=1)
        products.append(jnp.dot(x, tiles, preferred_element_type=F32))
    for k, b in enumerate((0, 1, block_count - 2, block_count - 1)):
        for t in (0, 1):
            rows = pl.ds(pl.multiple_of(window_ref[t, b] * 8, 8), 8)
            send_ref[owner_ref[t, b], rows, :] += products[k][0:8, LANES * t : LANES * t + LANES]
    values = sum(
        jnp.dot(
            deltas[s].astype(BF16),
            jnp.where(block == 2 * cell + s, 1.0, 0.0).astype(BF16),
            preferred_element_type=F32,
        )
        for s in (0, 1)
    )
    values = jnp.concatenate([values, values], axis=1)
    lines = line_ref[...].astype(BF16)
    targets = owners_ref[...] * WINDOWS + windows_ref[...]
    targets = jnp.concatenate([targets[0:1], targets[1:2]], axis=1)
    targets = jnp.broadcast_to(targets, values.shape)
    owners = send_ref.shape[0]
    wide = 4
    outs = []
    for o in range(0, owners, wide):
        rows = [
            jnp.where(targets == w, values, 0.0)
            for w in range(o * WINDOWS, (o + wide) * WINDOWS)
        ]
        columns = jnp.dot(
            jnp.concatenate(rows, axis=0).astype(BF16), lines, preferred_element_type=F32
        )
        for k in range(wide):
            send_ref[o + k, 0:32, :] += columns[32 * k : 32 * k + 32]
        spot = pl.ds(o, wide)
        sem = sems.at[8 + o // wide]
        outs.append(pltpu.make_async_copy(send_ref.at[spot], send_hbm.at[spot], sem))
        outs[-1].start()
    for out in outs:
        out.wait()


def fix_edges(source, turns, route, own, scale, part, line, edges, weights):
    return pl.pallas_call(
        fix_kernel,
        out_shape=(pltpu.HBM(part.shape, F32), jax.ShapeDtypeStruct((4, 8, CS), F32)),
        in_specs=[smem()] * 4 + [vmem()] * 4 + [anywhere()] + [hbm()] * 3,
        out_specs=(hbm(), vmem()),
        scratch_shapes=[
            pltpu.VMEM((4, 8, CS), F32),
            pltpu.VMEM((4, 2, LANES, LANES), BF16),
            pltpu.VMEM(line.shape, F32),
            pltpu.VMEM(part.shape, F32),
            pltpu.SemaphoreType.DMA((8 + part.shape[0] // 4,)),
        ],
        compiler_params=params(10),
        cost_estimate=cost(2 * 1024 * 1024 * 128, 3 << 20),
        name="edge_fix",
    )(
        source,
        turns,
        *route,
        *route,
        own,
        scale,
        edges,
        in_hbm(part),
        in_hbm(line),
        in_hbm(weights),
    )


def place_kernel(
    u_hbm,
    v_hbm,
    step_x_hbm,
    step_y_hbm,
    coriolis_hbm,
    lift_hbm,
    far_hbm,
    near_hbm,
    delta_ref,
    out_hbm,
    u_ref,
    v_ref,
    step_x_ref,
    step_y_ref,
    coriolis_ref,
    lift_ref,
    far_ref,
    near_ref,
    out_ref,
    cols,
    sems,
    out_sems,
):
    loads = half_loads(
        (u_hbm, v_hbm, step_x_hbm, step_y_hbm, coriolis_hbm, lift_hbm, far_hbm, near_hbm),
        (u_ref, v_ref, step_x_ref, step_y_ref, coriolis_ref, lift_ref, far_ref, near_ref),
        sems,
    )
    for load in loads[0] + loads[1]:
        load.start()
    cols[...] = jnp.transpose(
        jnp.concatenate(
            [delta_ref[0], delta_ref[1], jnp.zeros((LANES - 16, CS), F32)], axis=0
        )
    )
    lane = lax.broadcasted_iota(jnp.int32, (CHUNK, CS), 1)

    def put(r0, r, value):
        rows = pl.ds(r0, CHUNK)
        sides = cols[rows, :]
        left = jnp.where(lane == 0, sides[:, r : r + 1], 0.0)
        right = jnp.where(lane == CS - 1, sides[:, 8 + r : 9 + r], 0.0)
        out_ref[r // 4, r % 4, rows, :] = value + (left + right)

    inner = stencil_step(u_ref, v_ref, lift_ref, step_x_ref, step_y_ref, coriolis_ref, put)
    terms = outer_terms(lax.rem(lax.axis_index("lev"), 2), lift_ref, far_ref, near_ref)

    def step(c, carry):
        inner(c, carry)
        rows = pl.ds(pl.multiple_of(c * CHUNK, CHUNK), CHUNK)
        for comp, level, value in terms(rows):
            out_ref[comp, level, rows, :] += value
        return carry

    first, second = pl.ds(0, SPLIT * CHUNK), pl.ds(SPLIT * CHUNK, CS - SPLIT * CHUNK)
    outs = [
        pltpu.make_async_copy(out_ref.at[:, :, rows], out_hbm.at[:, :, rows], out_sems.at[k])
        for k, rows in enumerate((first, second))
    ]
    ends = ((0, SPLIT, 0, 2), (SPLIT, CS // CHUNK, CS - 1, 3))
    for h, (start, stop, line, side) in enumerate(ends):
        for load in loads[h]:
            load.wait()
        lax.fori_loop(start, stop, step, 0)
        for comp in (0, 1):
            for level in range(4):
                r = comp * 4 + level
                out_ref[comp, level, line : line + 1, :] += delta_ref[side, r : r + 1, :]
        outs[h].start()
    for out in outs:
        out.wait()


def place(fields, delta):
    return pl.pallas_call(
        place_kernel,
        out_shape=pltpu.HBM((2, 4, CS, CS), F32),
        in_specs=[hbm()] * len(fields) + [vmem()],
        out_specs=hbm(),
        scratch_shapes=[pltpu.VMEM(x.shape, F32) for x in fields]
        + [
            pltpu.VMEM((2, 4, CS, CS), F32),
            pltpu.VMEM((CS, LANES), F32),
            pltpu.SemaphoreType.DMA((2, len(fields))),
            pltpu.SemaphoreType.DMA((2,)),
        ],
        compiler_params=params(14),
        cost_estimate=cost(1 << 20, 8 << 20),
        name="place",
    )(*[in_hbm(x) for x in fields], delta)


def finish_kernel(got_ref, out_ref):
    total = got_ref[0]
    for d in range(1, got_ref.shape[0]):
        total = total + got_ref[d]
    for w in range(WINDOWS):
        share = total[8 * w : 8 * w + 8] / jnp.maximum(total[32 + w : 33 + w], 1.0)
        out_ref[0, :, LANES * w : LANES * w + LANES] = share[0:4]
        out_ref[1, :, LANES * w : LANES * w + LANES] = share[4:8]


def finish(got):
    return pl.pallas_call(
        finish_kernel,
        out_shape=jax.ShapeDtypeStruct((2, 4, WINDOWS * LANES), F32),
        in_specs=[vmem()],
        out_specs=vmem(),
        compiler_params=params(4),
        cost_estimate=cost(1000, 1 << 20),
        name="finish",
    )(got)


def per_device(
    wind_u,
    wind_v,
    vertical,
    spacing_x,
    spacing_y,
    coriolis,
    edge_source,
    edge_turns,
    route_owner,
    route_window,
    remap_weights,
):
    owners = lax.axis_size("sub")
    groups = lax.axis_size("lev")
    edges, own, far, near = take_edges(wind_u, wind_v, owners)
    odds = range(1, groups - 1, 2)
    far = lax.ppermute(far, "lev", [(i, i + 1) for i in odds] + [(i + 1, i) for i in odds])
    near = lax.ppermute(near, "lev", [(i, i ^ 1) for i in range(groups)])
    edges = lax.all_to_all(edges, "sub", split_axis=0, concat_axis=0, tiled=True)
    route = (route_owner.T, route_window.T)
    fields = (wind_u, wind_v, spacing_x, spacing_y, coriolis, vertical)
    blocks, scale, lift, held = inner_tendencies(fields, remap_weights)
    part, line, far, near = remap_inner(
        route, blocks, held, lift, far, near, remap_weights, owners
    )
    send, delta = fix_edges(
        edge_source, edge_turns, route, own, scale, part, line, edges, remap_weights
    )
    got = lax.all_to_all(send, "sub", split_axis=0, concat_axis=0, tiled=True)
    return place(fields + (far, near), delta), finish(in_vmem(got))


def solution(mesh):
    placed = (
        P("lev", "sub", None),
        P("lev", "sub", None),
        P("lev", "sub", None),
        P("sub", None),
        P("sub", None),
        P("sub", None),
        P("sub", None),
        P("sub", None),
        P("sub", None),
        P("sub", None),
        P("sub", None, None, None),
    )
    return jax.shard_map(
        per_device,
        mesh=mesh,
        in_specs=placed,
        out_specs=(P(None, "lev", "sub", None), P(None, "lev", "sub")),
        check_vma=False,
    )
```

time: 75.5 us -> 60.6 us (0.80)
  the two profiles are of different devices: /device:TPU:1 before, /device:TPU:0 now
where the time goes in v2:
time: 60.6 us; the launch traced here: 60.2 us
  Pallas kernels  31 us (51%)
  starting transfers between devices  22 us (36%)
  waiting for transfers between devices  6.39 us (11%)
  between operations  0.81 us (1%)
    pallas_call x1, Pallas kernels, remap_inner(): pl.pallas_call(remap_kernel, out_shape=(pltpu.HBM((owners, 40, LANES), F3...  11.3 us
    all_to_all x1, starting transfers between devices, per_device(): lax.all_to_all(edges, 'sub', split_axis=0, concat_axis=0, tiled=True)  8.4 us
    all_to_all x1, starting transfers between devices, per_device(): got = lax.all_to_all(send, 'sub', split_axis=0, concat_axis=0, tiled=True)  8.26 us
    all_to_all x1, waiting for transfers between devices, per_device(): got = lax.all_to_all(send, 'sub', split_axis=0, concat_axis=0, tiled=True)  6.38 us
    pallas_call x1, Pallas kernels, place(): pl.pallas_call(place_kernel, out_shape=pltpu.HBM((2, 4, CS, CS), F32), in...  6.12 us
    pallas_call x1, Pallas kernels, inner_tendencies(): pl.pallas_call(stencil_kernel, out_shape=(pltpu.VMEM((CS * 16, LANES), F3...  5.79 us
    ppermute x1, starting transfers between devices, per_device(): near = lax.ppermute(near, 'lev', [(i, i ^ 1) for i in range(groups)])  4.69 us
    pallas_call x1, Pallas kernels, fix_edges(): pl.pallas_call(fix_kernel, out_shape=(pltpu.HBM(part.shape, F32), jax.Sha...  3.87 us
  transfers between devices with their start and end apart: 4, of which 1 were waited for; matrix products, arithmetic and copies ran while one was open for 0% of the time, Pallas kernels for 39%

profile of v2, /device:TPU:0, one launch (start us, length us, event | category | flops | bytes accessed | tf_op | source)
XLA Modules:
  0.0 60.2 jit_solution(18390412872447704985)
XLA Ops:
  0.6 3.3 %edges.1 = (f32[32,32,256]{2,1,0:T(8,128)}, f32[32,256]{1,0:T(8,128)}, f32[2,256,256]{2,1,0:T(8,128)}, f32[2,256,256]{2,1,0:T(8,128)}) custom-call(f32[4,256,256]{2,1,0:T(8,128)} %u_hbm.3, f32[4,256,256]{2,1,0:T(8,128)} %v_hbm.3), custom_call_target="tpu_custom_call" | custom-call | flops 1000 | bytes 4194304 | tf_op jit(solution)/shard_map/edges/pallas_call | solution.py:101
  3.9 0.7 %collective-permute-start = (f32[2,256,256]{2,1,0:T(8,128)}, f32[2,256,256]{2,1,0:T(8,128)S(1)}, u32[]{:S(2)}, u32[]{:S(2)}) collective-permute-start(f32[2,256,256]{2,1,0:T(8,128)} %get-tuple-element.19), channel_id=1, source_target_pairs={{1,2},{2,1},{5,6},{6,5},{9,10},{10,9},{13,14},{14,13},{17,18},{18,... | collective-permute-start | bytes 1572872 | tf_op jit(solution)/shard_map/ppermute | solution.py:742
  4.6 4.7 %collective-permute-start.1 = (f32[2,256,256]{2,1,0:T(8,128)}, f32[2,256,256]{2,1,0:T(8,128)S(1)}, u32[]{:S(2)}, u32[]{:S(2)}) collective-permute-start(f32[2,256,256]{2,1,0:T(8,128)} %get-tuple-element.20), channel_id=1, source_target_pairs={{0,1},{1,0},{2,3},{3,2},{4,5},{5,4},{6,7},{7,6},{8,9},{9,8},{10,11... | collective-permute-start | bytes 1572872 | tf_op jit(solution)/shard_map/ppermute | solution.py:743
  9.3 8.4 %all-to-all-start = ((f32[32,32,256]{2,1,0:T(8,128)}), f32[32,32,256]{2,1,0:T(8,128)}, u32[]{:S(2)}, u32[]{:S(2)}) async-start(f32[32,32,256]{2,1,0:T(8,128)} %get-tuple-element.25), calls=%async_computation | async-start | bytes 2097152 | tf_op jit(solution)/shard_map/all_to_all | solution.py:744
  17.7 0.0 copy-start.1
  17.7 0.0 copy-start.2
  17.7 5.8 %stencil.1 = (f32[4096,128]{1,0:T(8,128)S(1)}, f32[8,256]{1,0:T(8,128)}, f32[4,256,256]{2,1,0:T(8,128)S(1)}, bf16[128,2,128,128]{3,2,1,0:T(8,128)(2,1)S(1)}) custom-call(f32[4,256,256]{2,1,0:T(8,128)} %u_hbm.3, f32[4,256,256]{2,1,0:T(8,128)} %v_hbm.3, f32[256,256]{1,0:T(8,128)} %step_x_hbm.3, f32[256,256]{1,0:T(8,128)} %step_y_hbm.3, ...), custom_call_target="tpu_custom_call" | custom-call | tf_op jit(solution)/shard_map/stencil/pallas_call | solution.py:262
  23.5 0.0 collective-permute-done.far_ref
  23.5 0.0 collective-permute-done.1.near_ref
  23.5 0.0 copy-done.1
  23.6 0.0 copy-done.2
  23.6 0.0 copy-start
  23.6 0.0 copy-start.3
  23.6 0.0 copy-start.4
  23.6 0.0 copy-start.5
  23.6 11.3 %remap.1 = (f32[32,40,128]{2,1,0:T(8,128)}, f32[1024,128]{1,0:T(8,128)}, f32[2,256,256]{2,1,0:T(8,128)}, f32[2,256,256]{2,1,0:T(8,128)}) custom-call(s32[2,512]{1,0:T(2,128)S(1)} %bitcast.2, s32[2,512]{1,0:T(2,128)S(1)} %bitcast.5, f32[4096,128]{1,0:T(8,128)S(1)} %get-tuple-element.16.blocks_in, bf16[128,2,128,128]{3,2,1,0:T(8,128)(2,1)S(1)} %get-tuple-element.17.held_ref, ...), custom_call_target="tpu_custom_call" | custom-call | flops 999999986991104 | bytes 1099511627776 | tf_op jit(solution)/shard_map/remap/pallas_call | solution.py:416
  34.9 0.0 all-to-all-done.edges_any
  34.9 0.0 copy-done
  34.9 0.0 copy-done.3
  34.9 0.0 copy-done.4
  34.9 0.0 copy-done.5
  34.9 3.9 %edge_fix.1 = (f32[32,40,128]{2,1,0:T(8,128)}, f32[4,8,256]{2,1,0:T(8,128)S(1)}) custom-call(s32[1,4]{1,0:T(1,128)S(1)} %copy-done.4, s32[1,4]{1,0:T(1,128)S(1)} %copy-done.5, s32[2,512]{1,0:T(2,128)S(1)} %bitcast.3, s32[2,512]{1,0:T(2,128)S(1)} %bitcast.6, s32[2,512]{1,0:T(2,128)S(1)} %bitcast.4, s32[2,512]{1,0:T(2,128)S(1)} %bitcast.7, ...), custom_call_target="tpu_custom_call" | custom-call | flops 268435456 | bytes 3145728 | tf_op jit(solution)/shard_map/edge_fix/pallas_call | solution.py:581
  38.8 8.3 %all-to-all-start.1 = ((f32[32,40,128]{2,1,0:T(8,128)}), f32[32,40,128]{2,1,0:T(8,128)S(1)}, u32[]{:S(2)}, u32[]{:S(2)}) async-start(f32[32,40,128]{2,1,0:T(8,128)} %get-tuple-element.29), calls=%async_computation.1 | async-start | bytes 1310720 | tf_op jit(solution)/shard_map/all_to_all | solution.py:754
  47.1 6.1 %place.1 = f32[2,4,256,256]{3,2,1,0:T(8,128)} custom-call(f32[4,256,256]{2,1,0:T(8,128)} %u_hbm.3, f32[4,256,256]{2,1,0:T(8,128)} %v_hbm.3, f32[256,256]{1,0:T(8,128)} %step_x_hbm.3, f32[256,256]{1,0:T(8,128)} %step_y_hbm.3, f32[256,256]{1,0:T(8,128)} %coriolis_hbm.3, f32[4,256,256]{2,1,0:T(8,128)} %lift_hbm.3, f32[2,256,256]{2,1,0:T(8,128)} %get-tuple-element.21.far_hbm, ...), custom_call_target="tpu_custom_call" | custom-call | flops 1048576 | bytes 8388608 | tf_op jit(solution)/shard_map/place/pallas_call | solution.py:685
  53.2 6.4 %all-to-all-done.1.got_ref = f32[32,40,128]{2,1,0:T(8,128)S(1)} async-done(((f32[32,40,128]{2,1,0:T(8,128)}), f32[32,40,128]{2,1,0:T(8,128)S(1)}, u32[]{:S(2)}, u32[]{:S(2)}) %all-to-all-start.1) | async-done | bytes 655392 | tf_op jit(solution)/shard_map/all_to_all | solution.py:754
  59.6 0.7 %finish.1 = f32[2,4,512]{2,1,0:T(4,128)} custom-call(f32[32,40,128]{2,1,0:T(8,128)S(1)} %all-to-all-done.1.got_ref), custom_call_target="tpu_custom_call" | custom-call | flops 1000 | bytes 1048576 | tf_op jit(solution)/shard_map/finish/pallas_call | solution.py:714
Async XLA Ops:
  3.9 19.6 %collective-permute-start = (f32[2,256,256]{2,1,0:T(8,128)}, f32[2,256,256]{2,1,0:T(8,128)S(1)}, u32[]{:S(2)}, u32[]{:S(2)}) collective-permute-start(f32[2,256,256]{2,1,0:T(8,128)} %get-tuple-element.19), channel_id=1, source_target_pairs={{1,2},{2,1},{5,6},{6,5},{9,10},{10,9},{13,14},{14,13},{17,18},{18,... | collective-permute-start | bytes 1572872 | tf_op jit(solution)/shard_map/ppermute | solution.py:742
  4.6 18.9 %collective-permute-start.1 = (f32[2,256,256]{2,1,0:T(8,128)}, f32[2,256,256]{2,1,0:T(8,128)S(1)}, u32[]{:S(2)}, u32[]{:S(2)}) collective-permute-start(f32[2,256,256]{2,1,0:T(8,128)} %get-tuple-element.20), channel_id=1, source_target_pairs={{0,1},{1,0},{2,3},{3,2},{4,5},{5,4},{6,7},{7,6},{8,9},{9,8},{10,11... | collective-permute-start | bytes 1572872 | tf_op jit(solution)/shard_map/ppermute | solution.py:743
  9.3 25.6 %all-to-all-start = ((f32[32,32,256]{2,1,0:T(8,128)}), f32[32,32,256]{2,1,0:T(8,128)}, u32[]{:S(2)}, u32[]{:S(2)}) async-start(f32[32,32,256]{2,1,0:T(8,128)} %get-tuple-element.25), calls=%async_computation | async-start | bytes 2097152 | tf_op jit(solution)/shard_map/all_to_all | solution.py:744
  17.7 5.8 %copy-start.1 = (s32[512,2]{0,1:T(2,128)S(1)}, s32[512,2]{0,1:T(2,128)}, u32[]{:S(2)}) copy-start(s32[512,2]{0,1:T(2,128)} %param.19) | copy-start | bytes 12292
  17.7 5.8 %copy-start.2 = (s32[512,2]{0,1:T(2,128)S(1)}, s32[512,2]{0,1:T(2,128)}, u32[]{:S(2)}) copy-start(s32[512,2]{0,1:T(2,128)} %param.20) | copy-start | bytes 12292
  23.6 11.3 %copy-start = (f32[32,256]{1,0:T(8,128)S(1)}, f32[32,256]{1,0:T(8,128)}, u32[]{:S(2)}) copy-start(f32[32,256]{1,0:T(8,128)} %get-tuple-element.23.own_ref) | copy-start | bytes 98308
  23.6 11.3 %copy-start.3 = (f32[8,256]{1,0:T(8,128)S(1)}, f32[8,256]{1,0:T(8,128)}, u32[]{:S(2)}) copy-start(f32[8,256]{1,0:T(8,128)} %get-tuple-element.24.scale_ref) | copy-start | bytes 24580
  23.6 11.3 %copy-start.4 = (s32[1,4]{1,0:T(1,128)S(1)}, s32[1,4]{1,0:T(1,128)}, u32[]{:S(2)}) copy-start(s32[1,4]{1,0:T(1,128)} %source_ref.1) | copy-start | bytes 52
  23.6 11.3 %copy-start.5 = (s32[1,4]{1,0:T(1,128)S(1)}, s32[1,4]{1,0:T(1,128)}, u32[]{:S(2)}) copy-start(s32[1,4]{1,0:T(1,128)} %turns_ref.1) | copy-start | bytes 52
  38.8 20.8 %all-to-all-start.1 = ((f32[32,40,128]{2,1,0:T(8,128)}), f32[32,40,128]{2,1,0:T(8,128)S(1)}, u32[]{:S(2)}, u32[]{:S(2)}) async-start(f32[32,40,128]{2,1,0:T(8,128)} %get-tuple-element.29), calls=%async_computation.1 | async-start | bytes 1310720 | tf_op jit(solution)/shard_map/all_to_all | solution.py:754

commit v3 on v2

--- a/solution.py
+++ b/solution.py
@@ -10,9 +10,10 @@
 LANES = 128
 CHUNK = 16
 ACCS = 4
-GROUP = 64
+GROUP = 32
 PIECE = 32
-HELD = 128
+WIDE = 4
+HELD = 160
 SPLIT = CS // CHUNK // 2 - 1
 QUARTERS = 4
 F32 = jnp.float32
@@ -52,7 +53,23 @@
 
 
 def edge_kernel(
-    wind_u, wind_v, edges_ref, own_ref, far_ref, near_ref, u_ref, v_ref, held, in_sems, out_sems
+    wind_u,
+    wind_v,
+    step_x_hbm,
+    step_y_hbm,
+    coriolis_hbm,
+    edges_ref,
+    own_ref,
+    far_ref,
+    near_ref,
+    u_ref,
+    v_ref,
+    step_x_ref,
+    step_y_ref,
+    coriolis_ref,
+    held,
+    in_sems,
+    out_sems,
 ):
     loads, sends = [], []
     order = [(comp, level) for level in (0, 3, 1, 2) for comp in (0, 1)]
@@ -62,6 +79,13 @@
             pltpu.make_async_copy(winds[comp].at[level], refs[comp].at[level], in_sems.at[k])
         )
     for load in loads:
+        load.start()
+    sources, dests = (step_x_hbm, step_y_hbm, coriolis_hbm), (step_x_ref, step_y_ref, coriolis_ref)
+    steps = [
+        pltpu.make_async_copy(source, dest, in_sems.at[8 + k])
+        for k, (source, dest) in enumerate(zip(sources, dests))
+    ]
+    for load in steps:
         load.start()
     lane = lax.broadcasted_iota(jnp.int32, (CS, LANES), 1)
     columns = jnp.zeros((CS, LANES), F32)
@@ -79,25 +103,25 @@
             at = 0 if side == 0 else CS - 1
             column = ref[level, :, pl.ds(at, 1)]
             columns = jnp.where(lane == side * 8 + comp * 4 + level, column, columns)
-    parts = [jnp.transpose(columns)[0:16, :]]
-    for at in (0, CS - 1):
-        for ref in refs:
-            parts.append(ref[:, at, :])
-    edges = jnp.concatenate(parts, axis=0)
     owners = held.shape[0]
-    for d in range(owners):
-        held[d] = edges
+    lines = [ref[:, at, :] for at in (0, CS - 1) for ref in refs]
+    for k, rows in ((1, lines), (0, None)):
+        edges = jnp.concatenate(rows, axis=0) if rows else jnp.transpose(columns)[0:16, :]
+        spot = pl.ds(16 * k, 16)
+        for d in range(owners):
+            held[d, spot, :] = edges
+        for n in (0, 1):
+            part = pl.ds(n * (owners // 2), owners // 2)
+            source, dest = held.at[part, spot], edges_ref.at[part, spot]
+            sends.append(pltpu.make_async_copy(source, dest, out_sems.at[5 + 2 * k + n]))
+            sends[-1].start()
     sends.append(pltpu.make_async_copy(held.at[0], own_ref, out_sems.at[4]))
     sends[-1].start()
-    for k in range(4):
-        part = pl.ds(k * (owners // 4), owners // 4)
-        sends.append(pltpu.make_async_copy(held.at[part], edges_ref.at[part], out_sems.at[k + 5]))
-        sends[-1].start()
-    for send in sends:
-        send.wait()
-
-
-def take_edges(wind_u, wind_v, owners):
+    for copy in sends + steps:
+        copy.wait()
+
+
+def take_edges(fields, owners):
     return pl.pallas_call(
         edge_kernel,
         out_shape=(
@@ -105,20 +129,19 @@
             pltpu.HBM((32, CS), F32),
             pltpu.HBM((2, CS, CS), F32),
             pltpu.HBM((2, CS, CS), F32),
-        ),
-        in_specs=[hbm(), hbm()],
-        out_specs=(hbm(),) * 4,
+        )
+        + tuple(pltpu.VMEM(x.shape, F32) for x in fields),
+        in_specs=[hbm()] * 5,
+        out_specs=(hbm(),) * 4 + (vmem(),) * 5,
         scratch_shapes=[
-            pltpu.VMEM((4, CS, CS), F32),
-            pltpu.VMEM((4, CS, CS), F32),
             pltpu.VMEM((owners, 32, CS), F32),
-            pltpu.SemaphoreType.DMA((8,)),
+            pltpu.SemaphoreType.DMA((11,)),
             pltpu.SemaphoreType.DMA((9,)),
         ],
         compiler_params=params(5),
         cost_estimate=cost(1000, 4 << 20),
         name="edges",
-    )(in_hbm(wind_u), in_hbm(wind_v))
+    )(*[in_hbm(x) for x in fields])
 
 
 def spread(blocks, r0, r, value):
@@ -201,30 +224,21 @@
 
 
 def stencil_kernel(
-    u_hbm,
-    v_hbm,
-    step_x_hbm,
-    step_y_hbm,
-    coriolis_hbm,
+    u_ref,
+    v_ref,
+    step_x_ref,
+    step_y_ref,
+    coriolis_ref,
     lift_hbm,
     weights_hbm,
     blocks,
     scale_ref,
     lift_ref,
     held_ref,
-    u_ref,
-    v_ref,
-    step_x_ref,
-    step_y_ref,
-    coriolis_ref,
     field_sems,
     sems,
 ):
-    loads = half_loads(
-        (u_hbm, v_hbm, step_x_hbm, step_y_hbm, coriolis_hbm, lift_hbm),
-        (u_ref, v_ref, step_x_ref, step_y_ref, coriolis_ref, lift_ref),
-        field_sems,
-    )
+    loads = half_loads((lift_hbm,), (lift_ref,), field_sems)
     for load in loads[0] + loads[1]:
         load.start()
     copies = []
@@ -238,10 +252,10 @@
         load.wait()
     for copy in copies:
         copy.start()
-    lax.fori_loop(0, SPLIT, step, 0)
+    lax.fori_loop(0, CS // CHUNK // 2, step, 0)
     for load in loads[1]:
         load.wait()
-    lax.fori_loop(SPLIT, CS // CHUNK, step, 0)
+    lax.fori_loop(CS // CHUNK // 2, CS // CHUNK, step, 0)
     side = lax.broadcasted_iota(jnp.int32, (CS, LANES), 1)
     columns = jnp.where(side == 0, step_x_ref[:, 0:1], step_x_ref[:, CS - 1 : CS])
     steps = jnp.concatenate(
@@ -258,7 +272,7 @@
         copy.wait()
 
 
-def inner_tendencies(fields, weights):
+def inner_tendencies(fields, lift, weights):
     return pl.pallas_call(
         stencil_kernel,
         out_shape=(
@@ -267,21 +281,16 @@
             pltpu.VMEM((4, CS, CS), F32),
             pltpu.VMEM((HELD,) + weights.shape[1:], BF16),
         ),
-        in_specs=[hbm()] * 7,
+        in_specs=[vmem()] * 5 + [hbm()] * 2,
         out_specs=(vmem(),) * 4,
         scratch_shapes=[
-            pltpu.VMEM((4, CS, CS), F32),
-            pltpu.VMEM((4, CS, CS), F32),
-            pltpu.VMEM((CS, CS), F32),
-            pltpu.VMEM((CS, CS), F32),
-            pltpu.VMEM((CS, CS), F32),
-            pltpu.SemaphoreType.DMA((2, 6)),
+            pltpu.SemaphoreType.DMA((2, 1)),
             pltpu.SemaphoreType.DMA((HELD // PIECE,)),
         ],
         compiler_params=params(10),
         cost_estimate=cost(0, 0),
         name="stencil",
-    )(*[in_hbm(x) for x in fields], in_hbm(weights))
+    )(*[in_vmem(x) for x in fields], in_hbm(lift), in_hbm(weights))
 
 
 def outer_terms(odd, lift_ref, far_ref, near_ref):
@@ -557,7 +566,7 @@
     targets = jnp.concatenate([targets[0:1], targets[1:2]], axis=1)
     targets = jnp.broadcast_to(targets, values.shape)
     owners = send_ref.shape[0]
-    wide = 4
+    wide = WIDE
     outs = []
     for o in range(0, owners, wide):
         rows = [
@@ -588,7 +597,7 @@
             pltpu.VMEM((4, 2, LANES, LANES), BF16),
             pltpu.VMEM(line.shape, F32),
             pltpu.VMEM(part.shape, F32),
-            pltpu.SemaphoreType.DMA((8 + part.shape[0] // 4,)),
+            pltpu.SemaphoreType.DMA((8 + part.shape[0] // WIDE,)),
         ],
         compiler_params=params(10),
         cost_estimate=cost(2 * 1024 * 1024 * 128, 3 << 20),
@@ -737,14 +746,14 @@
 ):
     owners = lax.axis_size("sub")
     groups = lax.axis_size("lev")
-    edges, own, far, near = take_edges(wind_u, wind_v, owners)
+    fields = (wind_u, wind_v, spacing_x, spacing_y, coriolis)
+    edges, own, far, near, *held_fields = take_edges(fields, owners)
     odds = range(1, groups - 1, 2)
     far = lax.ppermute(far, "lev", [(i, i + 1) for i in odds] + [(i + 1, i) for i in odds])
     near = lax.ppermute(near, "lev", [(i, i ^ 1) for i in range(groups)])
     edges = lax.all_to_all(edges, "sub", split_axis=0, concat_axis=0, tiled=True)
     route = (route_owner.T, route_window.T)
-    fields = (wind_u, wind_v, spacing_x, spacing_y, coriolis, vertical)
-    blocks, scale, lift, held = inner_tendencies(fields, remap_weights)
+    blocks, scale, lift, held = inner_tendencies(held_fields, vertical, remap_weights)
     part, line, far, near = remap_inner(
         route, blocks, held, lift, far, near, remap_weights, owners
     )
@@ -752,7 +761,7 @@
         edge_source, edge_turns, route, own, scale, part, line, edges, remap_weights
     )
     got = lax.all_to_all(send, "sub", split_axis=0, concat_axis=0, tiled=True)
-    return place(fields + (far, near), delta), finish(in_vmem(got))
+    return place(fields + (vertical, far, near), delta), finish(in_vmem(got))
 
 
 def solution(mesh):

time: 60.6 us -> 60.1 us (level)
  transfers between devices with their start and end apart: 4 -> 4, of which waited for: 1 -> 2; matrix products, arithmetic and copies ran while one was open for 0% -> 0% of each run, Pallas kernels for 39% -> 38%
where the time goes in v3:
time: 60.1 us; the launch traced here: 59.6 us
  Pallas kernels  30.4 us (51%)
  starting transfers between devices  21.6 us (36%)
  waiting for transfers between devices  6.89 us (11%)
  between operations  0.78 us (1%)
    pallas_call x1, Pallas kernels, remap_inner(): pl.pallas_call(remap_kernel, out_shape=(pltpu.HBM((owners, 40, LANES), F3...  10.7 us
    all_to_all x1, starting transfers between devices, per_device(): lax.all_to_all(edges, 'sub', split_axis=0, concat_axis=0, tiled=True)  8.4 us
    all_to_all x1, starting transfers between devices, per_device(): got = lax.all_to_all(send, 'sub', split_axis=0, concat_axis=0, tiled=True)  7.79 us
    all_to_all x1, waiting for transfers between devices, per_device(): got = lax.all_to_all(send, 'sub', split_axis=0, concat_axis=0, tiled=True)  6.38 us
    pallas_call x1, Pallas kernels, place(): pl.pallas_call(place_kernel, out_shape=pltpu.HBM((2, 4, CS, CS), F32), in...  6.12 us
    pallas_call x1, Pallas kernels, inner_tendencies(): pl.pallas_call(stencil_kernel, out_shape=(pltpu.VMEM((CS * 16, LANES), F3...  5.79 us
    ppermute x1, starting transfers between devices, per_device(): near = lax.ppermute(near, 'lev', [(i, i ^ 1) for i in range(groups)])  4.69 us
    pallas_call x1, Pallas kernels, fix_edges(): pl.pallas_call(fix_kernel, out_shape=(pltpu.HBM(part.shape, F32), jax.Sha...  3.87 us
  transfers between devices with their start and end apart: 4, of which 2 were waited for; matrix products, arithmetic and copies ran while one was open for 0% of the time, Pallas kernels for 38%

profile of v3, /device:TPU:0, one launch (start us, length us, event | category | flops | bytes accessed | tf_op | source)
XLA Modules:
  0.0 59.6 jit_solution(3528841250728647980)
XLA Ops:
  0.6 3.2 %edges.1 = (f32[32,32,256]{2,1,0:T(8,128)}, f32[32,256]{1,0:T(8,128)}, f32[2,256,256]{2,1,0:T(8,128)}, f32[2,256,256]{2,1,0:T(8,128)}, f32[4,256,256]{2,1,0:T(8,...) custom-call(f32[4,256,256]{2,1,0:T(8,128)} %u_hbm.1, ...), custom_call_target="tpu_custom_call" | custom-call | flops 1000 | bytes 4194304 | tf_op jit(solution)/shard_map/edges/pallas_call | solution.py:125
  3.8 0.7 %collective-permute-start = (f32[2,256,256]{2,1,0:T(8,128)}, f32[2,256,256]{2,1,0:T(8,128)S(1)}, u32[]{:S(2)}, u32[]{:S(2)}) collective-permute-start(f32[2,256,256]{2,1,0:T(8,128)} %get-tuple-element.29), channel_id=1, source_target_pairs={{1,2},{2,1},{5,6},{6,5},{9,10},{10,9},{13,14},{14,13},{17,18},{18,... | collective-permute-start | bytes 1572872 | tf_op jit(solution)/shard_map/ppermute | solution.py:752
  4.5 4.7 %collective-permute-start.1 = (f32[2,256,256]{2,1,0:T(8,128)}, f32[2,256,256]{2,1,0:T(8,128)}, u32[]{:S(2)}, u32[]{:S(2)}) collective-permute-start(f32[2,256,256]{2,1,0:T(8,128)} %get-tuple-element.30), channel_id=1, source_target_pairs={{0,1},{1,0},{2,3},{3,2},{4,5},{5,4},{6,7},{7,6},{8,9},{9,8},{10,11... | collective-permute-start | bytes 1572872 | tf_op jit(solution)/shard_map/ppermute | solution.py:753
  9.2 8.4 %all-to-all-start = ((f32[32,32,256]{2,1,0:T(8,128)}), f32[32,32,256]{2,1,0:T(8,128)}, u32[]{:S(2)}, u32[]{:S(2)}) async-start(f32[32,32,256]{2,1,0:T(8,128)} %get-tuple-element.35), calls=%async_computation | async-start | bytes 2097152 | tf_op jit(solution)/shard_map/all_to_all | solution.py:754
  17.6 0.0 copy-start.1
  17.6 0.0 copy-start.2
  17.6 5.8 %stencil.1 = (f32[4096,128]{1,0:T(8,128)S(1)}, f32[8,256]{1,0:T(8,128)}, f32[4,256,256]{2,1,0:T(8,128)S(1)}, bf16[160,2,128,128]{3,2,1,0:T(8,128)(2,1)S(1)}) custom-call(f32[4,256,256]{2,1,0:T(8,128)S(1)} %get-tuple-element.21.u_ref, f32[4,256,256]{2,1,0:T(8,128)S(1)} %get-tuple-element.22.v_ref, f32[256,256]{1,0:T(8,128)S(1)} %get-tuple-element.23.step_x_ref, ...), custom_call_target="tpu_custom_call" | custom-call | tf_op jit(solution)/shard_map/stencil/pallas_call | solution.py:276
  23.4 0.0 collective-permute-done.far_ref
  23.5 0.0 collective-permute-done.1.near_ref
  23.5 0.0 copy-done.1
  23.5 0.0 copy-done.2
  23.5 0.0 copy-start
  23.5 0.0 copy-start.3
  23.5 0.0 copy-start.4
  23.5 0.0 copy-start.5
  23.5 10.7 %remap.1 = (f32[32,40,128]{2,1,0:T(8,128)}, f32[1024,128]{1,0:T(8,128)}, f32[2,256,256]{2,1,0:T(8,128)}, f32[2,256,256]{2,1,0:T(8,128)}) custom-call(s32[2,512]{1,0:T(2,128)S(1)} %bitcast.2, s32[2,512]{1,0:T(2,128)S(1)} %bitcast.5, f32[4096,128]{1,0:T(8,128)S(1)} %get-tuple-element.26.blocks_in, bf16[160,2,128,128]{3,2,1,0:T(8,128)(2,1)S(1)} %get-tuple-element.27.held_ref, ...), custom_call_target="tpu_custom_call" | custom-call | flops 999999986991104 | bytes 1099511627776 | tf_op jit(solution)/shard_map/remap/pallas_call | solution.py:425
  34.3 0.5 all-to-all-done.edges_any
  34.8 0.0 copy-done
  34.8 0.0 copy-done.3
  34.8 0.0 copy-done.4
  34.8 0.0 copy-done.5
  34.8 3.9 %edge_fix.1 = (f32[32,40,128]{2,1,0:T(8,128)}, f32[4,8,256]{2,1,0:T(8,128)S(1)}) custom-call(s32[1,4]{1,0:T(1,128)S(1)} %copy-done.4, s32[1,4]{1,0:T(1,128)S(1)} %copy-done.5, s32[2,512]{1,0:T(2,128)S(1)} %bitcast.3, s32[2,512]{1,0:T(2,128)S(1)} %bitcast.6, s32[2,512]{1,0:T(2,128)S(1)} %bitcast.4, s32[2,512]{1,0:T(2,128)S(1)} %bitcast.7, ...), custom_call_target="tpu_custom_call" | custom-call | flops 268435456 | bytes 3145728 | tf_op jit(solution)/shard_map/edge_fix/pallas_call | solution.py:590
  38.7 7.8 %all-to-all-start.1 = ((f32[32,40,128]{2,1,0:T(8,128)}), f32[32,40,128]{2,1,0:T(8,128)S(1)}, u32[]{:S(2)}, u32[]{:S(2)}) async-start(f32[32,40,128]{2,1,0:T(8,128)} %get-tuple-element.39), calls=%async_computation.1 | async-start | bytes 1310720 | tf_op jit(solution)/shard_map/all_to_all | solution.py:763
  46.5 6.1 %place.1 = f32[2,4,256,256]{3,2,1,0:T(8,128)} custom-call(f32[4,256,256]{2,1,0:T(8,128)} %u_hbm.1, f32[4,256,256]{2,1,0:T(8,128)} %v_hbm.1, f32[256,256]{1,0:T(8,128)} %step_x_hbm.3, f32[256,256]{1,0:T(8,128)} %step_y_hbm.3, f32[256,256]{1,0:T(8,128)} %coriolis_hbm.3, f32[4,256,256]{2,1,0:T(8,128)} %lift_hbm.3, f32[2,256,256]{2,1,0:T(8,128)} %get-tuple-element.31.far_hbm, ...), custom_call_target="tpu_custom_call" | custom-call | flops 1048576 | bytes 8388608 | tf_op jit(solution)/shard_map/place/pallas_call | solution.py:694
  52.6 6.4 %all-to-all-done.1.got_ref = f32[32,40,128]{2,1,0:T(8,128)S(1)} async-done(((f32[32,40,128]{2,1,0:T(8,128)}), f32[32,40,128]{2,1,0:T(8,128)S(1)}, u32[]{:S(2)}, u32[]{:S(2)}) %all-to-all-start.1) | async-done | bytes 655392 | tf_op jit(solution)/shard_map/all_to_all | solution.py:763
  59.0 0.7 %finish.1 = f32[2,4,512]{2,1,0:T(4,128)} custom-call(f32[32,40,128]{2,1,0:T(8,128)S(1)} %all-to-all-done.1.got_ref), custom_call_target="tpu_custom_call" | custom-call | flops 1000 | bytes 1048576 | tf_op jit(solution)/shard_map/finish/pallas_call | solution.py:723
Async XLA Ops:
  3.8 19.6 %collective-permute-start = (f32[2,256,256]{2,1,0:T(8,128)}, f32[2,256,256]{2,1,0:T(8,128)S(1)}, u32[]{:S(2)}, u32[]{:S(2)}) collective-permute-start(f32[2,256,256]{2,1,0:T(8,128)} %get-tuple-element.29), channel_id=1, source_target_pairs={{1,2},{2,1},{5,6},{6,5},{9,10},{10,9},{13,14},{14,13},{17,18},{18,... | collective-permute-start | bytes 1572872 | tf_op jit(solution)/shard_map/ppermute | solution.py:752
  4.5 18.9 %collective-permute-start.1 = (f32[2,256,256]{2,1,0:T(8,128)}, f32[2,256,256]{2,1,0:T(8,128)}, u32[]{:S(2)}, u32[]{:S(2)}) collective-permute-start(f32[2,256,256]{2,1,0:T(8,128)} %get-tuple-element.30), channel_id=1, source_target_pairs={{0,1},{1,0},{2,3},{3,2},{4,5},{5,4},{6,7},{7,6},{8,9},{9,8},{10,11... | collective-permute-start | bytes 1572872 | tf_op jit(solution)/shard_map/ppermute | solution.py:753
  9.2 25.6 %all-to-all-start = ((f32[32,32,256]{2,1,0:T(8,128)}), f32[32,32,256]{2,1,0:T(8,128)}, u32[]{:S(2)}, u32[]{:S(2)}) async-start(f32[32,32,256]{2,1,0:T(8,128)} %get-tuple-element.35), calls=%async_computation | async-start | bytes 2097152 | tf_op jit(solution)/shard_map/all_to_all | solution.py:754
  17.6 5.8 %copy-start.1 = (s32[512,2]{0,1:T(2,128)S(1)}, s32[512,2]{0,1:T(2,128)}, u32[]{:S(2)}) copy-start(s32[512,2]{0,1:T(2,128)} %param.19) | copy-start | bytes 12292
  17.6 5.8 %copy-start.2 = (s32[512,2]{0,1:T(2,128)S(1)}, s32[512,2]{0,1:T(2,128)}, u32[]{:S(2)}) copy-start(s32[512,2]{0,1:T(2,128)} %param.20) | copy-start | bytes 12292
  23.5 11.3 %copy-start = (f32[32,256]{1,0:T(8,128)S(1)}, f32[32,256]{1,0:T(8,128)}, u32[]{:S(2)}) copy-start(f32[32,256]{1,0:T(8,128)} %get-tuple-element.33.own_ref) | copy-start | bytes 98308
  23.5 11.3 %copy-start.3 = (f32[8,256]{1,0:T(8,128)S(1)}, f32[8,256]{1,0:T(8,128)}, u32[]{:S(2)}) copy-start(f32[8,256]{1,0:T(8,128)} %get-tuple-element.34.scale_ref) | copy-start | bytes 24580
  23.5 11.3 %copy-start.4 = (s32[1,4]{1,0:T(1,128)S(1)}, s32[1,4]{1,0:T(1,128)}, u32[]{:S(2)}) copy-start(s32[1,4]{1,0:T(1,128)} %source_ref.1) | copy-start | bytes 52
  23.5 11.3 %copy-start.5 = (s32[1,4]{1,0:T(1,128)S(1)}, s32[1,4]{1,0:T(1,128)}, u32[]{:S(2)}) copy-start(s32[1,4]{1,0:T(1,128)} %turns_ref.1) | copy-start | bytes 52
  38.7 20.3 %all-to-all-start.1 = ((f32[32,40,128]{2,1,0:T(8,128)}), f32[32,40,128]{2,1,0:T(8,128)S(1)}, u32[]{:S(2)}, u32[]{:S(2)}) async-start(f32[32,40,128]{2,1,0:T(8,128)} %get-tuple-element.39), calls=%async_computation.1 | async-start | bytes 1310720 | tf_op jit(solution)/shard_map/all_to_all | solution.py:763

commit v4 on v3

--- a/solution.py
+++ b/solution.py
@@ -10,10 +10,9 @@
 LANES = 128
 CHUNK = 16
 ACCS = 4
-GROUP = 32
+GROUP = 64
 PIECE = 32
 WIDE = 4
-HELD = 160
 SPLIT = CS // CHUNK // 2 - 1
 QUARTERS = 4
 F32 = jnp.float32
@@ -55,18 +54,12 @@
 def edge_kernel(
     wind_u,
     wind_v,
-    step_x_hbm,
-    step_y_hbm,
-    coriolis_hbm,
     edges_ref,
     own_ref,
     far_ref,
     near_ref,
     u_ref,
     v_ref,
-    step_x_ref,
-    step_y_ref,
-    coriolis_ref,
     held,
     in_sems,
     out_sems,
@@ -79,13 +72,6 @@
             pltpu.make_async_copy(winds[comp].at[level], refs[comp].at[level], in_sems.at[k])
         )
     for load in loads:
-        load.start()
-    sources, dests = (step_x_hbm, step_y_hbm, coriolis_hbm), (step_x_ref, step_y_ref, coriolis_ref)
-    steps = [
-        pltpu.make_async_copy(source, dest, in_sems.at[8 + k])
-        for k, (source, dest) in enumerate(zip(sources, dests))
-    ]
-    for load in steps:
         load.start()
     lane = lax.broadcasted_iota(jnp.int32, (CS, LANES), 1)
     columns = jnp.zeros((CS, LANES), F32)
@@ -117,7 +103,7 @@
             sends[-1].start()
     sends.append(pltpu.make_async_copy(held.at[0], own_ref, out_sems.at[4]))
     sends[-1].start()
-    for copy in sends + steps:
+    for copy in sends:
         copy.wait()
 
 
@@ -131,8 +117,8 @@
             pltpu.HBM((2, CS, CS), F32),
         )
         + tuple(pltpu.VMEM(x.shape, F32) for x in fields),
-        in_specs=[hbm()] * 5,
-        out_specs=(hbm(),) * 4 + (vmem(),) * 5,
+        in_specs=[hbm()] * 2,
+        out_specs=(hbm(),) * 4 + (vmem(),) * 2,
         scratch_shapes=[
             pltpu.VMEM((owners, 32, CS), F32),
             pltpu.SemaphoreType.DMA((11,)),
@@ -223,42 +209,88 @@
     return stencil
 
 
-def stencil_kernel(
+def outer_terms(odd, lift_ref, far_ref, near_ref):
+    sides = ((far_ref, 3 * odd, odd), (near_ref, 3 - 3 * odd, 1 - odd))
+
+    def terms(rows):
+        out = []
+        for ref, level, top in sides:
+            lift = lift_ref[level, rows, :] * jnp.where(top == 1, -0.5, 0.5)
+            out += [(comp, level, lift * ref[comp, rows, :]) for comp in (0, 1)]
+        return out
+
+    return terms
+
+
+def remap_kernel(
+    owner_hbm,
+    window_hbm,
     u_ref,
     v_ref,
+    step_x_hbm,
+    step_y_hbm,
+    coriolis_hbm,
+    lift_hbm,
+    far_any,
+    near_any,
+    weights_hbm,
+    scale_ref,
+    part_hbm,
+    line_hbm,
+    far_hbm,
+    near_hbm,
+    part_ref,
+    blocks,
+    line_ref,
+    owner_ref,
+    window_ref,
     step_x_ref,
     step_y_ref,
     coriolis_ref,
-    lift_hbm,
-    weights_hbm,
-    blocks,
-    scale_ref,
     lift_ref,
-    held_ref,
-    field_sems,
-    sems,
+    far_ref,
+    near_ref,
+    weights_ref,
+    *rest,
 ):
-    loads = half_loads((lift_hbm,), (lift_ref,), field_sems)
-    for load in loads[0] + loads[1]:
-        load.start()
-    copies = []
-    for k in range(HELD // PIECE):
-        part = pl.ds(k * PIECE, PIECE)
-        copies.append(pltpu.make_async_copy(weights_hbm.at[part], held_ref.at[part], sems.at[k]))
+    accs, (sems, in_sems, field_sems) = rest[:ACCS], rest[ACCS:]
+    block_count = weights_hbm.shape[0]
+    steps = block_count // GROUP
+    lines = GROUP // 2
+    loads = half_loads(
+        (step_x_hbm, step_y_hbm, coriolis_hbm, lift_hbm),
+        (step_x_ref, step_y_ref, coriolis_ref, lift_ref),
+        field_sems,
+    )
+    firsts = [
+        pltpu.make_async_copy(owner_hbm, owner_ref, in_sems.at[2]),
+        pltpu.make_async_copy(window_hbm, window_ref, in_sems.at[5 + QUARTERS]),
+        pltpu.make_async_copy(far_any, far_ref, in_sems.at[0]),
+        pltpu.make_async_copy(near_any, near_ref, in_sems.at[1]),
+    ]
+    for copy in loads[0] + loads[1] + firsts:
+        copy.start()
+
+    def load(c):
+        part = pl.ds(c * PIECE, PIECE)
+        return pltpu.make_async_copy(weights_hbm.at[part], weights_ref.at[part], sems.at[c])
+
+    for acc in accs:
+        acc[...] = jnp.zeros_like(acc)
     step = stencil_step(
         u_ref, v_ref, lift_ref, step_x_ref, step_y_ref, coriolis_ref, lambda *at: spread(blocks, *at)
     )
-    for load in loads[0]:
-        load.wait()
-    for copy in copies:
-        copy.start()
+    for copy in loads[0]:
+        copy.wait()
+    for c in range(block_count // PIECE):
+        load(c).start()
     lax.fori_loop(0, CS // CHUNK // 2, step, 0)
-    for load in loads[1]:
-        load.wait()
+    for copy in loads[1]:
+        copy.wait()
     lax.fori_loop(CS // CHUNK // 2, CS // CHUNK, step, 0)
     side = lax.broadcasted_iota(jnp.int32, (CS, LANES), 1)
     columns = jnp.where(side == 0, step_x_ref[:, 0:1], step_x_ref[:, CS - 1 : CS])
-    steps = jnp.concatenate(
+    ends = jnp.concatenate(
         [
             jnp.transpose(columns)[0:2],
             step_y_ref[0:1, :],
@@ -267,78 +299,9 @@
         ],
         axis=0,
     )
-    scale_ref[...] = 0.5 / steps
-    for copy in copies:
+    scale_ref[...] = 0.5 / ends
+    for copy in firsts:
         copy.wait()
-
-
-def inner_tendencies(fields, lift, weights):
-    return pl.pallas_call(
-        stencil_kernel,
-        out_shape=(
-            pltpu.VMEM((CS * 16, LANES), F32),
-            pltpu.HBM((8, CS), F32),
-            pltpu.VMEM((4, CS, CS), F32),
-            pltpu.VMEM((HELD,) + weights.shape[1:], BF16),
-        ),
-        in_specs=[vmem()] * 5 + [hbm()] * 2,
-        out_specs=(vmem(),) * 4,
-        scratch_shapes=[
-            pltpu.SemaphoreType.DMA((2, 1)),
-            pltpu.SemaphoreType.DMA((HELD // PIECE,)),
-        ],
-        compiler_params=params(10),
-        cost_estimate=cost(0, 0),
-        name="stencil",
-    )(*[in_vmem(x) for x in fields], in_hbm(lift), in_hbm(weights))
-
-
-def outer_terms(odd, lift_ref, far_ref, near_ref):
-    sides = ((far_ref, 3 * odd, odd), (near_ref, 3 - 3 * odd, 1 - odd))
-
-    def terms(rows):
-        out = []
-        for ref, level, top in sides:
-            lift = lift_ref[level, rows, :] * jnp.where(top == 1, -0.5, 0.5)
-            out += [(comp, level, lift * ref[comp, rows, :]) for comp in (0, 1)]
-        return out
-
-    return terms
-
-
-def remap_kernel(
-    owner_ref,
-    window_ref,
-    blocks_in,
-    held_ref,
-    lift_ref,
-    far_ref,
-    near_ref,
-    weights_hbm,
-    part_hbm,
-    line_hbm,
-    far_hbm,
-    near_hbm,
-    part_ref,
-    blocks,
-    line_ref,
-    rest_ref,
-    *rest,
-):
-    accs, (sems, in_sems) = rest[:ACCS], rest[ACCS:]
-    block_count = weights_hbm.shape[0]
-    steps = block_count // GROUP
-    held_steps = HELD // GROUP
-    lines = GROUP // 2
-
-    def load(c):
-        source = weights_hbm.at[pl.ds(HELD + c * PIECE, PIECE)]
-        return pltpu.make_async_copy(source, rest_ref.at[pl.ds(c * PIECE, PIECE)], sems.at[c])
-
-    for acc in accs:
-        acc[...] = jnp.zeros_like(acc)
-    for c in range((block_count - HELD) // PIECE):
-        load(c).start()
     outs = [
         pltpu.make_async_copy(far_ref, far_hbm, in_sems.at[3]),
         pltpu.make_async_copy(near_ref, near_hbm, in_sems.at[4]),
@@ -349,20 +312,20 @@
     terms = outer_terms(odd, lift_ref, far_ref, near_ref)
 
     def levels(r0):
-        part = pl.ds(pl.multiple_of(r0 * 16, 128), 128)
-        blocks[part, :] = blocks_in[part, :]
         for comp, level, value in terms(pl.ds(r0, 8)):
             for h in (0, 1):
                 spot = pl.ds(r0 * 16 + 8 * h + comp * 4 + level, 8, stride=16)
                 half = value[:, LANES * h : LANES * h + LANES]
-                blocks[spot, :] = blocks_in[spot, :] + half
+                blocks[spot, :] = blocks[spot, :] + half
 
     row = lax.broadcasted_iota(jnp.int32, (8, LANES), 0)
     lane = lax.broadcasted_iota(jnp.int32, (8, LANES), 1)
     ones = jnp.where(row == 0, 1.0, 0.0)
     extra = [jnp.where((row == 1) & (lane == q), 1.0, ones) for q in (0, LANES - 1)]
 
-    def remap(c, weights_ref, first_block):
+    def remap(c, carry):
+        for k in range(GROUP // PIECE):
+            load(c * (GROUP // PIECE) + k).wait()
         for k in range(lines // 8):
             levels(pl.multiple_of(c * lines + 8 * k, 8))
         parts, targets = [], []
@@ -370,8 +333,7 @@
             b = c * GROUP + k
             x = blocks[pl.ds(pl.multiple_of(b * 8, 8), 8), :]
             x = jnp.concatenate([x, extra[k & 1]], axis=0).astype(BF16)
-            here = b - first_block
-            tiles = jnp.concatenate([weights_ref[here, 0], weights_ref[here, 1]], axis=1)
+            tiles = jnp.concatenate([weights_ref[b, 0], weights_ref[b, 1]], axis=1)
             product = jnp.dot(x, tiles, preferred_element_type=F32)
             for t in (0, 1):
                 half = product[:, LANES * t : LANES * t + LANES]
@@ -383,20 +345,10 @@
             olds = [accs[i - first][targets[i]] for i in here]
             for i, old in zip(here, olds):
                 accs[i - first][targets[i]] = old + parts[i]
-
-    def remap_held(c, carry):
-        remap(c, held_ref, 0)
         return carry
 
-    def remap_rest(c, carry):
-        for k in range(GROUP // PIECE):
-            load((c - held_steps) * (GROUP // PIECE) + k).wait()
-        remap(c, rest_ref, HELD)
-        return carry
-
-    lax.fori_loop(0, held_steps, remap_held, 0)
-    lax.fori_loop(held_steps, steps, remap_rest, 0)
-    line_out = pltpu.make_async_copy(line_ref, line_hbm, in_sems.at[2])
+    lax.fori_loop(0, steps, remap, 0)
+    line_out = pltpu.make_async_copy(line_ref, line_hbm, in_sems.at[6 + QUARTERS])
     line_out.start()
 
     def gather(o, carry):
@@ -420,35 +372,46 @@
         out.wait()
 
 
-def remap_inner(route, blocks, held, lift, far, near, weights, owners):
+def remap_inner(route, winds, fields, far, near, weights, owners):
     count = weights.shape[0]
     return pl.pallas_call(
         remap_kernel,
         out_shape=(
+            pltpu.HBM((8, CS), F32),
             pltpu.HBM((owners, 40, LANES), F32),
             pltpu.HBM((2 * count, LANES), F32),
             pltpu.HBM((2, CS, CS), F32),
             pltpu.HBM((2, CS, CS), F32),
         ),
-        in_specs=[smem()] * 2 + [vmem()] * 5 + [hbm()],
-        out_specs=(hbm(),) * 4,
+        in_specs=[hbm()] * 2 + [vmem()] * 2 + [hbm()] * 4 + [anywhere()] * 2 + [hbm()],
+        out_specs=(vmem(),) + (hbm(),) * 4,
         scratch_shapes=[
             pltpu.VMEM((owners, 40, LANES), F32),
-            pltpu.VMEM(blocks.shape, F32),
+            pltpu.VMEM((count * 8, LANES), F32),
             pltpu.VMEM((2 * count, LANES), F32),
-            pltpu.VMEM((count - HELD,) + weights.shape[1:], BF16),
+            pltpu.SMEM((2, count), jnp.int32),
+            pltpu.SMEM((2, count), jnp.int32),
+            pltpu.VMEM((CS, CS), F32),
+            pltpu.VMEM((CS, CS), F32),
+            pltpu.VMEM((CS, CS), F32),
+            pltpu.VMEM((4, CS, CS), F32),
+            pltpu.VMEM((2, CS, CS), F32),
+            pltpu.VMEM((2, CS, CS), F32),
+            pltpu.VMEM(weights.shape, BF16),
         ]
         + [pltpu.VMEM((owners * WINDOWS, 16, LANES), F32)] * ACCS
         + [
-            pltpu.SemaphoreType.DMA(((count - HELD) // PIECE,)),
-            pltpu.SemaphoreType.DMA((5 + QUARTERS,)),
+            pltpu.SemaphoreType.DMA((count // PIECE,)),
+            pltpu.SemaphoreType.DMA((7 + QUARTERS,)),
+            pltpu.SemaphoreType.DMA((2, 4)),
         ],
-        compiler_params=params(36),
+        compiler_params=params(48),
         cost_estimate=cost(10**15, 1 << 40),
-        name="remap",
+        name="stencil_remap",
     )(
-        *route,
-        *[in_vmem(x) for x in (blocks, held, lift)],
+        *[in_hbm(x) for x in route],
+        *[in_vmem(x) for x in winds],
+        *[in_hbm(x) for x in fields],
         far,
         near,
         in_hbm(weights),
@@ -476,20 +439,21 @@
     owners_ref,
     windows_ref,
     own_ref,
-    scale_ref,
+    scale_hbm,
     edges_any,
     part_hbm,
     line_hbm,
     weights_hbm,
     send_hbm,
     delta_ref,
+    scale_ref,
     got,
     ends,
     line_ref,
     send_ref,
     sems,
 ):
-    edge_copies, copies = [], []
+    edge_copies, copies = [pltpu.make_async_copy(scale_hbm, scale_ref, sems.at[8])], []
     for s in range(4):
         e = source_ref[0, s]
         spot = edges_any.at[e >> 2, pl.ds(pl.multiple_of((e & 3) * 8, 8), 8)]
@@ -579,7 +543,7 @@
         for k in range(wide):
             send_ref[o + k, 0:32, :] += columns[32 * k : 32 * k + 32]
         spot = pl.ds(o, wide)
-        sem = sems.at[8 + o // wide]
+        sem = sems.at[9 + o // wide]
         outs.append(pltpu.make_async_copy(send_ref.at[spot], send_hbm.at[spot], sem))
         outs[-1].start()
     for out in outs:
@@ -590,14 +554,15 @@
     return pl.pallas_call(
         fix_kernel,
         out_shape=(pltpu.HBM(part.shape, F32), jax.ShapeDtypeStruct((4, 8, CS), F32)),
-        in_specs=[smem()] * 4 + [vmem()] * 4 + [anywhere()] + [hbm()] * 3,
+        in_specs=[smem()] * 4 + [vmem()] * 3 + [hbm(), anywhere()] + [hbm()] * 3,
         out_specs=(hbm(), vmem()),
         scratch_shapes=[
+            pltpu.VMEM((8, CS), F32),
             pltpu.VMEM((4, 8, CS), F32),
             pltpu.VMEM((4, 2, LANES, LANES), BF16),
             pltpu.VMEM(line.shape, F32),
             pltpu.VMEM(part.shape, F32),
-            pltpu.SemaphoreType.DMA((8 + part.shape[0] // WIDE,)),
+            pltpu.SemaphoreType.DMA((9 + part.shape[0] // WIDE,)),
         ],
         compiler_params=params(10),
         cost_estimate=cost(2 * 1024 * 1024 * 128, 3 << 20),
@@ -608,7 +573,7 @@
         *route,
         *route,
         own,
-        scale,
+        in_hbm(scale),
         edges,
         in_hbm(part),
         in_hbm(line),
@@ -747,15 +712,14 @@
     owners = lax.axis_size("sub")
     groups = lax.axis_size("lev")
     fields = (wind_u, wind_v, spacing_x, spacing_y, coriolis)
-    edges, own, far, near, *held_fields = take_edges(fields, owners)
+    edges, own, far, near, *winds = take_edges(fields[:2], owners)
     odds = range(1, groups - 1, 2)
     far = lax.ppermute(far, "lev", [(i, i + 1) for i in odds] + [(i + 1, i) for i in odds])
     near = lax.ppermute(near, "lev", [(i, i ^ 1) for i in range(groups)])
     edges = lax.all_to_all(edges, "sub", split_axis=0, concat_axis=0, tiled=True)
     route = (route_owner.T, route_window.T)
-    blocks, scale, lift, held = inner_tendencies(held_fields, vertical, remap_weights)
-    part, line, far, near = remap_inner(
-        route, blocks, held, lift, far, near, remap_weights, owners
+    scale, part, line, far, near = remap_inner(
+        route, winds, fields[2:] + (vertical,), far, near, remap_weights, owners
     )
     send, delta = fix_edges(
         edge_source, edge_turns, route, own, scale, part, line, edges, remap_weights

time: 60.1 us -> 58.5 us (0.973)
  starting transfers between devices: 21.6 us -> 20 us
  waiting for transfers between devices: 6.89 us -> 8.44 us
  Pallas kernels: 30.4 us -> 28.9 us
    all_to_all x1, starting transfers between devices: 7.79 us -> 6.22 us  [per_device(): got = lax.all_to_all(send, 'sub', split_axis=0, concat_axis=0, tiled=True)]
    all_to_all x1, waiting for transfers between devices: 0.5 us -> 2.06 us  [per_device(): lax.all_to_all(edges, 'sub', split_axis=0, concat_axis=0, tiled=True)]
    pallas_call x2 -> x1, Pallas kernels: 16.5 us -> 15 us  [remap_inner(): pl.pallas_call(remap_kernel, out_shape=(pltpu.HBM((8, CS), F32), pltpu.HB...]
  transfers between devices with their start and end apart: 4 -> 4, of which waited for: 2 -> 2; matrix products, arithmetic and copies ran while one was open for 0% -> 0% of each run, Pallas kernels for 38% -> 36%
where the time goes in v4:
time: 58.5 us; the launch traced here: 58.1 us
  Pallas kernels  28.9 us (49%)
  starting transfers between devices  20 us (34%)
  waiting for transfers between devices  8.44 us (14%)
  between operations  0.76 us (1%)
    pallas_call x1, Pallas kernels, remap_inner(): pl.pallas_call(remap_kernel, out_shape=(pltpu.HBM((8, CS), F32), pltpu.HB...  15 us
    all_to_all x1, starting transfers between devices, per_device(): lax.all_to_all(edges, 'sub', split_axis=0, concat_axis=0, tiled=True)  8.41 us
    all_to_all x1, waiting for transfers between devices, per_device(): got = lax.all_to_all(send, 'sub', split_axis=0, concat_axis=0, tiled=True)  6.38 us
    all_to_all x1, starting transfers between devices, per_device(): got = lax.all_to_all(send, 'sub', split_axis=0, concat_axis=0, tiled=True)  6.22 us
    pallas_call x1, Pallas kernels, place(): pl.pallas_call(place_kernel, out_shape=pltpu.HBM((2, 4, CS, CS), F32), in...  6.12 us
    ppermute x1, starting transfers between devices, per_device(): near = lax.ppermute(near, 'lev', [(i, i ^ 1) for i in range(groups)])  4.69 us
    pallas_call x1, Pallas kernels, fix_edges(): pl.pallas_call(fix_kernel, out_shape=(pltpu.HBM(part.shape, F32), jax.Sha...  3.88 us
    pallas_call x1, Pallas kernels, take_edges(): pl.pallas_call(edge_kernel, out_shape=(pltpu.HBM((owners, 32, CS), F32),...  3.17 us
  transfers between devices with their start and end apart: 4, of which 2 were waited for; matrix products, arithmetic and copies ran while one was open for 0% of the time, Pallas kernels for 36%

profile of v4, /device:TPU:0, one launch (start us, length us, event | category | flops | bytes accessed | tf_op | source)
XLA Modules:
  0.0 58.1 jit_solution(12875085432083342609)
XLA Ops:
  0.6 3.2 %edges.1 = (f32[32,32,256]{2,1,0:T(8,128)}, f32[32,256]{1,0:T(8,128)}, f32[2,256,256]{2,1,0:T(8,128)}, f32[2,256,256]{2,1,0:T(8,128)}, f32[4,256,256]{2,1,0:T(8,128)S(1)}, /*index=5*/f32[4,256,256]{2,1,0:T(8,128)S(1)}) custom-call(f32[4,256,256]{2,1,0:T(8,128)} %u_hbm.1, f32[4,256,256]{2,1,0:T(8,128)} %v_hbm.1), custom_call_target="tpu_custom_call" | custom-call | flops 1000 | bytes 4194304 | tf_op jit(solution)/shard_map/edges/pallas_call | solution.py:111
  3.8 0.7 %collective-permute-start = (f32[2,256,256]{2,1,0:T(8,128)}, f32[2,256,256]{2,1,0:T(8,128)S(1)}, u32[]{:S(2)}, u32[]{:S(2)}) collective-permute-start(f32[2,256,256]{2,1,0:T(8,128)} %get-tuple-element.17), channel_id=1, source_target_pairs={{1,2},{2,1},{5,6},{6,5},{9,10},{10,9},{13,14},{14,13},{17,18},{18,... | collective-permute-start | bytes 1572872 | tf_op jit(solution)/shard_map/ppermute | solution.py:717
  4.5 4.7 %collective-permute-start.1 = (f32[2,256,256]{2,1,0:T(8,128)}, f32[2,256,256]{2,1,0:T(8,128)S(1)}, u32[]{:S(2)}, u32[]{:S(2)}) collective-permute-start(f32[2,256,256]{2,1,0:T(8,128)} %get-tuple-element.18), channel_id=1, source_target_pairs={{0,1},{1,0},{2,3},{3,2},{4,5},{5,4},{6,7},{7,6},{8,9},{9,8},{10,11... | collective-permute-start | bytes 1572872 | tf_op jit(solution)/shard_map/ppermute | solution.py:718
  9.2 8.4 %all-to-all-start = ((f32[32,32,256]{2,1,0:T(8,128)}), f32[32,32,256]{2,1,0:T(8,128)}, u32[]{:S(2)}, u32[]{:S(2)}) async-start(f32[32,32,256]{2,1,0:T(8,128)} %get-tuple-element.23), calls=%async_computation | async-start | bytes 2097152 | tf_op jit(solution)/shard_map/all_to_all | solution.py:719
  17.6 0.0 collective-permute-done.far_any
  17.6 0.0 collective-permute-done.1.near_any
  17.6 0.0 copy-start
  17.6 0.0 copy-start.1
  17.7 0.0 copy-start.2
  17.7 0.0 copy-start.3
  17.7 0.0 copy-start.4
  17.7 15.0 %stencil_remap.1 = (f32[8,256]{1,0:T(8,128)}, f32[32,40,128]{2,1,0:T(8,128)}, f32[1024,128]{1,0:T(8,128)}, f32[2,256,256]{2,1,0:T(8,128)}, f32[2,256,256]{2,1,0:T(8,128)}) custom-call(s32[2,512]{1,0:T(2,128)} %bitcast.2, s32[2,512]{1,0:T(2,128)} %bitcast.5, f32[4,256,256]{2,1,0:T(8,128)S(1)} %get-tuple-element.15.u_ref, ...), custom_call_target="tpu_custom_call" | custom-call | flops 999999986991104 | bytes 1099511627776 | tf_op jit(solution)/shard_map/stencil_remap/pallas_call | solution.py:377
  32.7 2.1 %all-to-all-done.edges_any = f32[32,32,256]{2,1,0:T(8,128)} async-done(((f32[32,32,256]{2,1,0:T(8,128)}), f32[32,32,256]{2,1,0:T(8,128)}, u32[]{:S(2)}, u32[]{:S(2)}) %all-to-all-start) | async-done | bytes 1048608 | tf_op jit(solution)/shard_map/all_to_all | solution.py:719
  34.8 0.0 copy-done
  34.8 0.0 copy-done.1
  34.8 0.0 copy-done.2
  34.8 0.0 copy-done.3
  34.8 0.0 copy-done.4
  34.8 3.9 %edge_fix.1 = (f32[32,40,128]{2,1,0:T(8,128)}, f32[4,8,256]{2,1,0:T(8,128)S(1)}) custom-call(s32[1,4]{1,0:T(1,128)S(1)} %copy-done.3, s32[1,4]{1,0:T(1,128)S(1)} %copy-done.4, s32[2,512]{1,0:T(2,128)S(1)} %bitcast.3, s32[2,512]{1,0:T(2,128)S(1)} %bitcast.6, s32[2,512]{1,0:T(2,128)S(1)} %bitcast.4, s32[2,512]{1,0:T(2,128)S(1)} %bitcast.7, ...), custom_call_target="tpu_custom_call" | custom-call | flops 268435456 | bytes 3145728 | tf_op jit(solution)/shard_map/edge_fix/pallas_call | solution.py:554
  38.7 6.2 %all-to-all-start.1 = ((f32[32,40,128]{2,1,0:T(8,128)}), f32[32,40,128]{2,1,0:T(8,128)S(1)}, u32[]{:S(2)}, u32[]{:S(2)}) async-start(f32[32,40,128]{2,1,0:T(8,128)} %get-tuple-element.27), calls=%async_computation.1 | async-start | bytes 1310720 | tf_op jit(solution)/shard_map/all_to_all | solution.py:727
  44.9 6.1 %place.1 = f32[2,4,256,256]{3,2,1,0:T(8,128)} custom-call(f32[4,256,256]{2,1,0:T(8,128)} %u_hbm.1, f32[4,256,256]{2,1,0:T(8,128)} %v_hbm.1, f32[256,256]{1,0:T(8,128)} %step_x_hbm.3, f32[256,256]{1,0:T(8,128)} %step_y_hbm.3, f32[256,256]{1,0:T(8,128)} %coriolis_hbm.3, f32[4,256,256]{2,1,0:T(8,128)} %lift_hbm.3, f32[2,256,256]{2,1,0:T(8,128)} %get-tuple-element.19.far_hbm, ...), custom_call_target="tpu_custom_call" | custom-call | flops 1048576 | bytes 8388608 | tf_op jit(solution)/shard_map/place/pallas_call | solution.py:659
  51.1 6.4 %all-to-all-done.1.got_ref = f32[32,40,128]{2,1,0:T(8,128)S(1)} async-done(((f32[32,40,128]{2,1,0:T(8,128)}), f32[32,40,128]{2,1,0:T(8,128)S(1)}, u32[]{:S(2)}, u32[]{:S(2)}) %all-to-all-start.1) | async-done | bytes 655392 | tf_op jit(solution)/shard_map/all_to_all | solution.py:727
  57.4 0.7 %finish.1 = f32[2,4,512]{2,1,0:T(4,128)} custom-call(f32[32,40,128]{2,1,0:T(8,128)S(1)} %all-to-all-done.1.got_ref), custom_call_target="tpu_custom_call" | custom-call | flops 1000 | bytes 1048576 | tf_op jit(solution)/shard_map/finish/pallas_call | solution.py:688
Async XLA Ops:
  3.8 13.8 %collective-permute-start = (f32[2,256,256]{2,1,0:T(8,128)}, f32[2,256,256]{2,1,0:T(8,128)S(1)}, u32[]{:S(2)}, u32[]{:S(2)}) collective-permute-start(f32[2,256,256]{2,1,0:T(8,128)} %get-tuple-element.17), channel_id=1, source_target_pairs={{1,2},{2,1},{5,6},{6,5},{9,10},{10,9},{13,14},{14,13},{17,18},{18,... | collective-permute-start | bytes 1572872 | tf_op jit(solution)/shard_map/ppermute | solution.py:717
  4.5 13.1 %collective-permute-start.1 = (f32[2,256,256]{2,1,0:T(8,128)}, f32[2,256,256]{2,1,0:T(8,128)S(1)}, u32[]{:S(2)}, u32[]{:S(2)}) collective-permute-start(f32[2,256,256]{2,1,0:T(8,128)} %get-tuple-element.18), channel_id=1, source_target_pairs={{0,1},{1,0},{2,3},{3,2},{4,5},{5,4},{6,7},{7,6},{8,9},{9,8},{10,11... | collective-permute-start | bytes 1572872 | tf_op jit(solution)/shard_map/ppermute | solution.py:718
  9.2 25.6 %all-to-all-start = ((f32[32,32,256]{2,1,0:T(8,128)}), f32[32,32,256]{2,1,0:T(8,128)}, u32[]{:S(2)}, u32[]{:S(2)}) async-start(f32[32,32,256]{2,1,0:T(8,128)} %get-tuple-element.23), calls=%async_computation | async-start | bytes 2097152 | tf_op jit(solution)/shard_map/all_to_all | solution.py:719
  17.6 17.1 %copy-start = (f32[32,256]{1,0:T(8,128)S(1)}, f32[32,256]{1,0:T(8,128)}, u32[]{:S(2)}) copy-start(f32[32,256]{1,0:T(8,128)} %get-tuple-element.21.own_ref) | copy-start | bytes 98308
  17.6 17.1 %copy-start.1 = (s32[512,2]{0,1:T(2,128)S(1)}, s32[512,2]{0,1:T(2,128)}, u32[]{:S(2)}) copy-start(s32[512,2]{0,1:T(2,128)} %param.19) | copy-start | bytes 12292
  17.7 17.1 %copy-start.2 = (s32[512,2]{0,1:T(2,128)S(1)}, s32[512,2]{0,1:T(2,128)}, u32[]{:S(2)}) copy-start(s32[512,2]{0,1:T(2,128)} %param.20) | copy-start | bytes 12292
  17.7 17.1 %copy-start.3 = (s32[1,4]{1,0:T(1,128)S(1)}, s32[1,4]{1,0:T(1,128)}, u32[]{:S(2)}) copy-start(s32[1,4]{1,0:T(1,128)} %source_ref.1) | copy-start | bytes 52
  17.7 17.1 %copy-start.4 = (s32[1,4]{1,0:T(1,128)S(1)}, s32[1,4]{1,0:T(1,128)}, u32[]{:S(2)}) copy-start(s32[1,4]{1,0:T(1,128)} %turns_ref.1) | copy-start | bytes 52
  38.7 18.7 %all-to-all-start.1 = ((f32[32,40,128]{2,1,0:T(8,128)}), f32[32,40,128]{2,1,0:T(8,128)S(1)}, u32[]{:S(2)}, u32[]{:S(2)}) async-start(f32[32,40,128]{2,1,0:T(8,128)} %get-tuple-element.27), calls=%async_computation.1 | async-start | bytes 1310720 | tf_op jit(solution)/shard_map/all_to_all | solution.py:727
